TPU v7x, 32 devices: a whole 2x2x4 slice. The times are simulated.
32 devices in a mesh: seq: 8 (over z, y), head: 4 (over x, core).
Axes of the slice: x: 2, y: 2, z: 4, core: 2. Of those that a mesh axis runs over, the one named last changes fastest.
Arguments:
- hidden_in: bfloat16 [2, 4096, 1024], P(None, 'seq'), may hold values from -6 to 6
- norm_gain: bfloat16 [1024], replicated, may hold values from 0.099609375 to 1.8984375
- query_weight: bfloat16 [1024, 512], P(None, 'head'), may hold values from -0.1875 to 0.1875
- keyvalue_matrix: bfloat16 [1024, 2, 128], replicated, may hold values from -0.1875 to 0.1875
- output_weight: bfloat16 [512, 1024], P('head'), may hold values from -2 to 2
- zgate_weight: bfloat16 [1024, 1536], P(None, 'head'), may hold values from -0.1875 to 0.1875
- inner_weight: bfloat16 [1024, 1536], P(None, 'head'), may hold values from -0.1875 to 0.1875
- state_weight: bfloat16 [1024, 256], replicated, may hold values from -0.1875 to 0.1875
- step_weight: bfloat16 [1024, 24], P(None, 'head'), may hold values from -0.5 to 0.5
- conv_inner: bfloat16 [4, 1536], P(None, 'head'), may hold values from -3 to 3
- conv_state: bfloat16 [4, 256], replicated, may hold values from -3 to 3
- step_bias: float32 [24], P('head'), may hold values from -4 to 0.5
- decay_log: float32 [24], P('head'), may hold values from -4.5 to 0.5
- skip_gain: float32 [24], P('head'), may hold values from 0.5 to 4
- ssm_gain: bfloat16 [1536], P('head'), may hold values from 0.099609375 to 1.8984375
- mixer_weight: bfloat16 [1536, 1024], P('head'), may hold values from -0.15625 to 0.15625
- mlp_gain: bfloat16 [1024], replicated, may hold values from 0.099609375 to 1.8984375
- gate_weight: bfloat16 [1024, 2048], P(None, 'head'), may hold values from -0.1875 to 0.1875
- up_weight: bfloat16 [1024, 2048], P(None, 'head'), may hold values from -0.1875 to 0.1875
- down_weight: bfloat16 [2048, 1024], P('head'), may hold values from -0.125 to 0.125
- grad_output: bfloat16 [2, 4096, 1024], P(None, 'seq'), may hold values from -6 to 6
Outputs:
- output: bfloat16 [2, 4096, 1024], P(None, 'seq')
- grad_input: float32 [2, 4096, 1024], P(None, 'seq')
- grad_norm_gain: float32 [1024], replicated
- grad_query_weight: float32 [1024, 512], P(None, 'head')
- grad_keyvalue_weight: float32 [1024, 2, 128], replicated
- grad_output_weight: float32 [512, 1024], P('head')
- grad_zgate_weight: float32 [1024, 1536], P(None, 'head')
- grad_inner_weight: float32 [1024, 1536], P(None, 'head')
- grad_state_weight: float32 [1024, 256], replicated
- grad_step_weight: float32 [1024, 24], P(None, 'head')
- grad_conv_inner: float32 [4, 1536], P(None, 'head')
- grad_conv_state: float32 [4, 256], replicated
- grad_step_bias: float32 [24], P('head')
- grad_decay_log: float32 [24], P('head')
- grad_skip_gain: float32 [24], P('head')
- grad_ssm_gain: float32 [1536], P('head')
- grad_mixer_weight: float32 [1536, 1024], P('head')
- grad_mlp_gain: float32 [1024], replicated
- grad_gate_weight: float32 [1024, 2048], P(None, 'head')
- grad_up_weight: float32 [1024, 2048], P(None, 'head')
- grad_down_weight: float32 [2048, 1024], P('head')
All inputs are finite; a program needn't handle non-finite values.
Results may differ from a plain program's by a relative error of at most 0.013.
The roundings to bfloat16 on the way count: a program that leaves them out, or rounds other values in their place, can miss the bound.
Values may be sent and summed in bfloat16 or wider, within the bound.
A program may use at most 256 MiB of HBM per device.

v0:
```python
import math

import jax
import jax.numpy as jnp
from jax import lax
from jax.sharding import PartitionSpec as P

HEADS = 8
KV_HEADS = 2
STATE = 128
SSM = 1536


HIGH_ACCURACY = lax.Precision.HIGHEST
EPSILON = 1e-05
ROPE_BASE = 100000000000.0
MASKED = -1e30


def passed_along(value, axis, steps):
    count = lax.axis_size(axis)
    first, last = (max(0, -steps), min(count, count - steps))
    return lax.ppermute(value, axis, [(source, source + steps) for source in range(first, last)])


def prefix(value, axis, join, neutral, backward):
    count, mine = (lax.axis_size(axis), lax.axis_index(axis))
    pieces = jax.tree.map(lambda part: lax.all_gather(part, axis), value)
    if backward:
        pieces = jax.tree.map(lambda part: part[::-1], pieces)
        mine = count - 1 - mine
    running = jax.tree.map(
        lambda part, zero: jnp.full_like(part, 0) + jnp.asarray(zero, part.dtype), value, neutral
    )

    def step(position, running):
        longer = join(running, jax.tree.map(lambda part: part[position], pieces))
        return jax.tree.map(lambda new, old: jnp.where(position < mine, new, old), longer, running)

    return lax.fori_loop(0, count - 1, step, running)


def matmul(left_operand, right_operand):
    return jnp.einsum(
        "std,de->ste", left_operand, right_operand, preferred_element_type=jnp.float32
    )


def matmul_back(grad, right_operand):
    return jnp.einsum("ste,de->std", grad, right_operand, preferred_element_type=jnp.float32)


def weight_grad(left_operand, grad):
    return jnp.einsum("std,ste->de", left_operand, grad, preferred_element_type=jnp.float32)


def rms_norm(values, gain):
    factor = lax.rsqrt(jnp.mean(values * values, axis=-1, keepdims=True) + EPSILON)
    return values * factor * gain


def rotate(values, positions):
    half = values.shape[-1] // 2
    freq = ROPE_BASE ** (-jnp.arange(half, dtype=jnp.float32) * 2.0 / values.shape[-1])
    angle = positions[:, None] * freq[None, :]
    cosine = jnp.cos(angle)[None, :, None, :]
    sine = jnp.sin(angle)[None, :, None, :]
    first = values[..., :half]
    second = values[..., half:]
    return jnp.concatenate(
        [first * cosine - second * sine, second * cosine + first * sine], axis=-1
    )


def block_scores(queries, keys, query_pos, key_pos, factor):
    scores = (
        jnp.einsum("sqhd,skd->shqk", queries, keys, preferred_element_type=jnp.float32) * factor
    )
    allowed = key_pos[None, :] <= query_pos[:, None]
    return jnp.where(allowed[None, None], scores, MASKED)


def conv_act(extended, conv_weight):
    rows = extended.shape[1] - (conv_weight.shape[0] - 1)
    summed = extended[:, 0:rows] * conv_weight[0]
    for tap in range(1, conv_weight.shape[0]):
        summed = summed + extended[:, tap : tap + rows] * conv_weight[tap]
    return jax.nn.silu(summed)


def ssm_inputs(extended, step_raw, conv_weight, step_bias, decay_log):
    activated = conv_act(extended, conv_weight)
    inner_width = activated.shape[-1] - 2 * STATE
    heads_here = step_raw.shape[-1]
    channels = activated[..., :inner_width].reshape(
        activated.shape[0], activated.shape[1], heads_here, inner_width // heads_here
    )
    writes = activated[..., inner_width : inner_width + STATE]
    reads = activated[..., inner_width + STATE :]
    step = jax.nn.softplus(step_raw + step_bias)
    logdecay = -step * jnp.exp(decay_log)
    return (channels, writes, reads, step, logdecay)


def intra(channels, writes, reads, step, running):
    rows = running.shape[1]
    lower = jnp.arange(rows, dtype=jnp.int32)[:, None] >= jnp.arange(rows, dtype=jnp.int32)[None, :]
    mask = lower[None, :, :, None]
    spread = running[:, :, None, :] - running[:, None, :, :]
    decay = jnp.where(mask, jnp.exp(jnp.where(mask, spread, 0.0)), 0.0)
    intersection = jnp.einsum("stn,sun->stu", reads, writes, precision=HIGH_ACCURACY)
    mixing = decay * intersection[..., None] * step[:, None, :, :]
    within = jnp.einsum("stuh,suhp->sthp", mixing, channels, precision=HIGH_ACCURACY)
    tail_weight = jnp.exp(running[:, -1:, :] - running) * step
    local = jnp.einsum("suh,suhp,sun->shpn", tail_weight, channels, writes, precision=HIGH_ACCURACY)
    return (within, local)


def inter(reads, running, state):
    return jnp.exp(running)[..., None] * jnp.einsum(
        "stn,shpn->sthp", reads, state, precision=HIGH_ACCURACY
    )


def ssm_full(extended, step_raw, conv_weight, step_bias, decay_log, skip_gain, state_in):
    channels, writes, reads, step, logdecay = ssm_inputs(
        extended, step_raw, conv_weight, step_bias, decay_log
    )
    running = jnp.cumsum(logdecay, axis=1)
    within, local = intra(channels, writes, reads, step, running)
    result = within + inter(reads, running, state_in) + skip_gain[:, None] * channels
    state_end = jnp.exp(running[:, -1])[:, :, None, None] * state_in + local
    return (result, state_end)


def chain(earlier, later):
    return (earlier[0] * later[0], later[0][:, :, None, None] * earlier[1] + later[1])


def on_device(
    hidden_in,
    norm_gain,
    query_weight,
    keyvalue_matrix,
    output_weight,
    zgate_weight,
    inner_weight,
    state_weight,
    step_weight,
    conv_inner,
    conv_state,
    step_bias,
    decay_log,
    skip_gain,
    ssm_gain,
    mixer_weight,
    mlp_gain,
    gate_weight,
    up_weight,
    down_weight,
    grad_output,
):
    sequences, rows, width = hidden_in.shape
    head_dim = keyvalue_matrix.shape[2] // 2
    heads_here = query_weight.shape[1] // head_dim
    group = HEADS // KV_HEADS
    factor = head_dim ** (-0.5)
    inner_width = inner_weight.shape[1]
    mamba_here = step_bias.shape[0]
    seq_index = lax.axis_index("seq")
    head_index = lax.axis_index("head")
    query_pos = seq_index * rows + jnp.arange(rows, dtype=jnp.int32)
    positions = query_pos.astype(jnp.float32)
    input_float = hidden_in.astype(jnp.float32)
    gain_one = norm_gain.astype(jnp.float32)
    normalized_input = rms_norm(input_float, gain_one).astype(jnp.bfloat16)
    query_raw = matmul(normalized_input, query_weight).reshape(
        sequences, rows, heads_here, head_dim
    )
    queries = rotate(query_raw, positions).astype(jnp.bfloat16)
    kv_index = head_index * heads_here // group
    own_weight = lax.dynamic_index_in_dim(keyvalue_matrix, kv_index, 1, keepdims=False)
    keyvalue_projected = matmul(normalized_input, own_weight)
    keys_own = rotate(keyvalue_projected[:, :, None, :head_dim], positions)[:, :, 0]
    keyvalue_own = jnp.concatenate([keys_own, keyvalue_projected[..., head_dim:]], axis=-1).astype(
        jnp.bfloat16
    )
    keyvalue_all = lax.all_gather(keyvalue_own, "seq", axis=1, tiled=True)
    length = keyvalue_all.shape[1]
    key_block = math.gcd(length, 512)
    blocks_needed = ((seq_index + 1) * rows + key_block - 1) // key_block

    def key_piece(index):
        start = index * key_block
        piece = lax.dynamic_slice_in_dim(keyvalue_all, start, key_block, 1)
        return (
            piece[..., :head_dim],
            piece[..., head_dim:],
            start + jnp.arange(key_block, dtype=jnp.int32),
        )

    def first_pass(index, carry):
        peak, total = carry
        keys, values, key_pos = key_piece(index)
        scores = block_scores(queries, keys, query_pos, key_pos, factor)
        new_peak = jnp.maximum(peak, jnp.max(scores, axis=-1))
        total = total * jnp.exp(peak - new_peak) + jnp.sum(
            jnp.exp(scores - new_peak[..., None]), axis=-1
        )
        return (new_peak, total)

    start_peak = jnp.full((sequences, heads_here, rows), MASKED, jnp.float32)
    peak, total = lax.fori_loop(
        0, blocks_needed, first_pass, (start_peak, jnp.zeros_like(start_peak))
    )
    log_total = peak + jnp.log(total)

    def second_pass(index, summed):
        keys, values, key_pos = key_piece(index)
        scores = block_scores(queries, keys, query_pos, key_pos, factor)
        probs = jnp.exp(scores - log_total[..., None]).astype(jnp.bfloat16)
        return summed + jnp.einsum(
            "shqk,skd->sqhd", probs, values, preferred_element_type=jnp.float32
        )

    attended_float = lax.fori_loop(
        0,
        blocks_needed,
        second_pass,
        jnp.zeros((sequences, rows, heads_here, head_dim), jnp.float32),
    )
    attended = attended_float.astype(jnp.bfloat16).reshape(sequences, rows, heads_here * head_dim)
    zgate = matmul(normalized_input, zgate_weight)
    inner = jnp.concatenate(
        [matmul(normalized_input, inner_weight), matmul(normalized_input, state_weight)], axis=-1
    )
    step_raw = matmul(normalized_input, step_weight)
    conv_weight = jnp.concatenate([conv_inner, conv_state], axis=1).astype(jnp.float32)
    taps = conv_weight.shape[0]
    before = passed_along(inner[:, rows - (taps - 1) :], "seq", 1)
    extended = jnp.concatenate([before, inner], axis=1)
    channels, writes, reads, step, logdecay = ssm_inputs(
        extended, step_raw, conv_weight, step_bias, decay_log
    )
    running = jnp.cumsum(logdecay, axis=1)
    within, local = intra(channels, writes, reads, step, running)
    decay_all = jnp.exp(running[:, -1])
    identity = (jnp.ones_like(decay_all), jnp.zeros_like(local))
    state_in = prefix((decay_all, local), "seq", chain, identity, False)[1]
    y_ssm = within + inter(reads, running, state_in) + skip_gain[:, None] * channels
    y_flat = y_ssm.reshape(sequences, rows, inner_width)
    gated = y_flat * jax.nn.silu(zgate)
    squares = lax.psum(jnp.sum(gated * gated, axis=-1), "head")
    ssm_factor = lax.rsqrt(squares / SSM + EPSILON)[..., None]
    gain_ssm = ssm_gain.astype(jnp.float32)
    ssm_normed = (gated * ssm_factor * gain_ssm).astype(jnp.bfloat16)
    branch_part = matmul(attended, output_weight) + matmul(ssm_normed, mixer_weight)
    quarter = rows // lax.axis_size("head")
    mixed_rows = lax.psum_scatter(branch_part, "head", scatter_dimension=1, tiled=True)
    hidden_rows = (
        lax.dynamic_slice_in_dim(input_float, head_index * quarter, quarter, 1) + mixed_rows
    )
    hidden = lax.all_gather(hidden_rows, "head", axis=1, tiled=True)
    gain_two = mlp_gain.astype(jnp.float32)
    normed_two = rms_norm(hidden, gain_two).astype(jnp.bfloat16)
    gate = matmul(normed_two, gate_weight)
    up = matmul(normed_two, up_weight)
    activated = (jax.nn.silu(gate) * up).astype(jnp.bfloat16)
    feed_part = matmul(activated, down_weight)
    feed_own = lax.psum_scatter(feed_part, "head", scatter_dimension=1, tiled=True)
    output_own = (hidden_rows + feed_own).astype(jnp.bfloat16)
    output = lax.all_gather(output_own, "head", axis=1, tiled=True)
    act_grad = matmul_back(grad_output, down_weight)
    grad_down = weight_grad(activated, grad_output)
    gate_pull = jax.vjp(lambda gate_in, up_in: jax.nn.silu(gate_in) * up_in, gate, up)[1]
    gate_grad, up_grad = gate_pull(act_grad)
    gate_grad = gate_grad.astype(jnp.bfloat16)
    up_grad = up_grad.astype(jnp.bfloat16)
    grad_gate = weight_grad(normed_two, gate_grad)
    grad_up = weight_grad(normed_two, up_grad)
    normed_two_grad = lax.psum(
        matmul_back(gate_grad, gate_weight) + matmul_back(up_grad, up_weight), "head"
    )
    norm_two_pull = jax.vjp(rms_norm, hidden, gain_two)[1]
    hidden_norm_grad, grad_gain_two = norm_two_pull(normed_two_grad)
    hidden_grad = grad_output.astype(jnp.float32) + hidden_norm_grad
    mixed_grad = hidden_grad.astype(jnp.bfloat16)
    grad_output_proj = weight_grad(attended, mixed_grad)
    attended_grad = (
        matmul_back(mixed_grad, output_weight)
        .astype(jnp.bfloat16)
        .reshape(sequences, rows, heads_here, head_dim)
    )
    grad_mixer = weight_grad(ssm_normed, mixed_grad)
    ssm_normed_grad = matmul_back(mixed_grad, mixer_weight)
    weighted = ssm_normed_grad * gain_ssm
    inner_total = lax.psum(jnp.sum(weighted * gated, axis=-1), "head")
    gated_grad = weighted * ssm_factor - gated * ssm_factor**3 * inner_total[..., None] / SSM
    grad_gain_ssm = jnp.sum(ssm_normed_grad * gated * ssm_factor, axis=(0, 1))
    gated_pull = jax.vjp(lambda y_in, z_in: y_in * jax.nn.silu(z_in), y_flat, zgate)[1]
    y_grad, zgate_grad = gated_pull(gated_grad)
    zgate_grad = zgate_grad.astype(jnp.bfloat16)
    grad_zgate = weight_grad(normalized_input, zgate_grad)
    y_grad_heads = y_grad.reshape(sequences, rows, mamba_here, inner_width // mamba_here)
    own_state_grad = jnp.einsum(
        "sth,stn,sthp->shpn", jnp.exp(running), reads, y_grad_heads, precision=HIGH_ACCURACY
    )
    state_grad = prefix((decay_all, own_state_grad), "seq", chain, identity, True)[1]
    ssm_pull = jax.vjp(
        ssm_full, extended, step_raw, conv_weight, step_bias, decay_log, skip_gain, state_in
    )[1]
    extended_grad, step_raw_grad, conv_grad, grad_step_bias, grad_decay_log, grad_skip, unused = (
        ssm_pull((y_grad_heads, state_grad))
    )
    before_grad = passed_along(extended_grad[:, : taps - 1], "seq", -1)
    inner_grad = extended_grad[:, taps - 1 :] + jnp.pad(
        before_grad, ((0, 0), (rows - (taps - 1), 0), (0, 0))
    )
    inner_own = inner_grad[..., :inner_width].astype(jnp.bfloat16)
    step_grad = step_raw_grad.astype(jnp.bfloat16)
    grad_inner = weight_grad(normalized_input, inner_own)
    grad_step = weight_grad(normalized_input, step_grad)
    delta = jnp.sum(attended_grad.astype(jnp.float32) * attended_float, axis=-1).transpose(0, 2, 1)

    def make_back_pass():

        def back_pass(index, carry):
            query_grad, keyvalue_grad = carry
            keys, values, key_pos = key_piece(index)
            scores = block_scores(queries, keys, query_pos, key_pos, factor)
            probs = jnp.exp(scores - log_total[..., None])
            probs_grad = jnp.einsum(
                "sqhd,skd->shqk", attended_grad, values, preferred_element_type=jnp.float32
            )
            scores_grad = (probs * (probs_grad - delta[..., None])).astype(jnp.bfloat16)
            query_grad = (
                query_grad
                + jnp.einsum(
                    "shqk,skd->sqhd", scores_grad, keys, preferred_element_type=jnp.float32
                )
                * factor
            )
            key_grad = (
                jnp.einsum(
                    "shqk,sqhd->skd", scores_grad, queries, preferred_element_type=jnp.float32
                )
                * factor
            )
            value_grad = jnp.einsum(
                "shqk,sqhd->skd",
                probs.astype(jnp.bfloat16),
                attended_grad,
                preferred_element_type=jnp.float32,
            )
            keyvalue_grad = lax.dynamic_update_slice_in_dim(
                keyvalue_grad,
                jnp.concatenate([key_grad, value_grad], axis=-1),
                index * key_block,
                1,
            )
            return (query_grad, keyvalue_grad)

        return back_pass

    query_zero = jnp.zeros((sequences, rows, heads_here, head_dim), jnp.float32)
    keyvalue_zero = jnp.zeros((sequences, length, 2 * head_dim), jnp.float32)
    query_grad, keyvalue_grad_all = lax.fori_loop(
        0, blocks_needed, make_back_pass(), (query_zero, keyvalue_zero)
    )
    keyvalue_grad_own = lax.psum_scatter(keyvalue_grad_all, "seq", scatter_dimension=1, tiled=True)
    key_raw_grad = rotate(keyvalue_grad_own[:, :, None, :head_dim], -positions)[:, :, 0]
    keyvalue_raw_grad = jnp.concatenate([key_raw_grad, keyvalue_grad_own[..., head_dim:]], axis=-1)
    chooser = (jnp.arange(KV_HEADS, dtype=jnp.int32) == kv_index).astype(jnp.float32)
    keyvalue_both = chooser[None, None, :, None] * keyvalue_raw_grad[:, :, None, :]
    query_raw_grad = (
        rotate(query_grad, -positions)
        .astype(jnp.bfloat16)
        .reshape(sequences, rows, heads_here * head_dim)
    )
    grad_query = weight_grad(normalized_input, query_raw_grad)
    normed_part = (
        matmul_back(query_raw_grad, query_weight)
        + matmul_back(zgate_grad, zgate_weight)
        + matmul_back(inner_own, inner_weight)
        + matmul_back(step_grad, step_weight)
    )
    normed_sum, keyvalue_sum, state_sum, conv_state_grad = lax.psum(
        (normed_part, keyvalue_both, inner_grad[..., inner_width:], conv_grad[:, inner_width:]),
        "head",
    )
    keyvalue_low = keyvalue_sum.astype(jnp.bfloat16)
    state_low = state_sum.astype(jnp.bfloat16)
    grad_keyvalue = jnp.einsum(
        "std,sthe->dhe", normalized_input, keyvalue_low, preferred_element_type=jnp.float32
    )
    grad_state = weight_grad(normalized_input, state_low)
    normed_grad = (
        normed_sum
        + jnp.einsum(
            "sthe,dhe->std", keyvalue_low, keyvalue_matrix, preferred_element_type=jnp.float32
        )
        + matmul_back(state_low, state_weight)
    )
    norm_one_pull = jax.vjp(rms_norm, input_float, gain_one)[1]
    input_norm_grad, grad_gain_one = norm_one_pull(normed_grad)
    grad_input = hidden_grad + input_norm_grad
    summed_grads = lax.psum(
        (
            grad_gain_one,
            grad_query,
            grad_keyvalue,
            grad_output_proj,
            grad_zgate,
            grad_inner,
            grad_state,
            grad_step,
            conv_grad[:, :inner_width],
            conv_state_grad,
            grad_step_bias,
            grad_decay_log,
            grad_skip,
            grad_gain_ssm,
            grad_mixer,
            grad_gain_two,
            grad_gate,
            grad_up,
            grad_down,
        ),
        "seq",
    )
    return (output, grad_input) + tuple(summed_grads)


def solution(mesh):
    placed = (
        P(None, "seq", None),
        P(),
        P(None, "head"),
        P(),
        P("head", None),
        P(None, "head"),
        P(None, "head"),
        P(),
        P(None, "head"),
        P(None, "head"),
        P(),
        P("head"),
        P("head"),
        P("head"),
        P("head"),
        P("head", None),
        P(),
        P(None, "head"),
        P(None, "head"),
        P("head", None),
        P(None, "seq", None),
    )
    return jax.shard_map(
        on_device,
        mesh=mesh,
        in_specs=placed,
        out_specs=(
            P(None, "seq", None),
            P(None, "seq", None),
            P(),
            P(None, "head"),
            P(),
            P("head", None),
            P(None, "head"),
            P(None, "head"),
            P(),
            P(None, "head"),
            P(None, "head"),
            P(),
            P("head"),
            P("head"),
            P("head"),
            P("head"),
            P("head", None),
            P(),
            P(None, "head"),
            P(None, "head"),
            P("head", None),
        ),
        check_vma=False,
    )
```

profile of v0, /device:TPU:0, one launch (start us, length us, event | category | flops | bytes accessed | tf_op | source)
XLA Modules:
  0.0 1327.9 jit_solution(17904906453927290885)
XLA Ops:
  25.9 5.6 collective-permute-start
  35.4 3.1 fusion.129
  40.3 7.2 reduce-window.14
  66.7 18.3 %all-gather = f32[16,1,6]{2,1,0:T(1,128)S(1)} all-gather(f32[2,1,6]{2,1,0:T(1,128)S(1)} %bitcast.457), channel_id=2, replica_groups=mesh['seq'=8,'head'=4] {'seq'}, dimensions={0}, use_global_device_ids=true | all-gather | bytes 432 | tf_op jit(solution)/shard_map/all_gather | solution.py:28
  86.8 2.9 maximum_maximum_fusion
  89.8 3.4 fusion.68
  97.5 4.4 fusion.155
  102.0 3.9 while.65
  107.3 5.0 while.66
  108.2 3.7 fusion.258
  114.1 3.7 fusion.162
  117.8 42.0 %all-gather.15.cloned.1.call-done = f32[16,6,64,128]{3,2,1,0:T(8,128)} async-done(((f32[2,6,64,128]{3,2,1,0:T(8,128)}), f32[16,6,64,128]{3,2,1,0:T(8,128)}) %all-gather.15.cloned.1.call-update) | async-done | bytes 3145744 | tf_op jit(solution)/shard_map/all_gather | solution.py:28
  159.7 13.8 %while.68 = (s32[]{:T(128)}, f32[2,6,64,128]{3,2,1,0:T(8,128)}, s32[]{:T(128)}, f32[8,2,6]{2,1,0:T(2,128)S(1)}, f32[8,2,6,64,128]{4,3,2,1,0:T(8,128)}, /*index=5*/s32[]{:T(128)}, s32[]{:T(128)}) while((s32[]{:T(128)}, f32[2,6,64,128]{3,2,1,0:T(8,128)}, s32[]{:T(128)}, f32[8,2,6]{2,1,0:T(2,128)S(1)}, ...), condition=%wide.region_10.11_spmd.clone, body=%wide.region_9.10_spmd.clone.sunk | while | flops 393220 | bytes 1179905 | solution.py:40
  176.1 17.7 %fusion.78 = f32[2,512,6,64]{1,3,2,0:T(8,128)S(1)} fusion(f32[2,512,6,64]{1,3,2,0:T(8,128)} %bitcast.429, f32[2,512,6,64]{1,3,2,0:T(8,128)S(1)} %fusion.137, f32[2,512,6]{1,2,0:T(8,128)} %copy.366, f32[2,512,512]{2,1,0:T(8,128)} %fusion.155, f32[2,512,6]{1,2,0:T(8,128)S(1)} %copy.362, pred[512,512]{1,0:T(8,128)(4,1)} %iota_compare_fusion, ...), kind=kOutput, calls=%fused_computation.146 | convolution fusion | flops 2433220608 | bytes 7151640 | tf_op jit(solution)/shard_map/stuh,suhp->sthp/dot_general | solution.py:113
  193.9 3.1 multiply_reduce_fusion.16
  197.0 5.7 psum.182
  202.7 6.3 convolution_add_fusion.1
  211.6 56.4 %reduce-scatter.4.cloned.1.call-done = f32[2,128,1024]{2,1,0:T(8,128)} async-done(((f32[2,512,1024]{2,1,0:T(8,128)}), f32[2,128,1024]{2,1,0:T(8,128)}) %reduce-scatter.4.cloned.1.call-update) | async-done | bytes 1048592 | tf_op jit(solution)/shard_map/reduce_scatter | solution.py:259
  271.0 34.4 %all-gather.11.cloned.1.call-done = f32[2,512,1024]{2,1,0:T(8,128)} async-done(((f32[2,128,1024]{2,1,0:T(8,128)}), f32[2,512,1024]{2,1,0:T(8,128)}) %all-gather.11.cloned.1.call-update) | async-done | bytes 4194320 | tf_op jit(solution)/shard_map/all_gather | solution.py:263
  313.6 3.1 multiply_convert_fusion.2
  318.0 3.3 convolution_add_fusion
  321.4 85.6 %all-reduce.22.cloned.1.call-done = f32[2,512,1024]{2,1,0:T(8,128)} async-done(((f32[2,512,1024]{2,1,0:T(8,128)}), f32[2,512,1024]{2,1,0:T(8,128)}) %all-reduce.22.cloned.1.call-update) | async-done | bytes 4194320 | tf_op jit(solution)/shard_map/psum | solution.py:281
  407.0 5.3 multiply_reduce_fusion.1
  415.6 2.9 multiply_reduce_fusion.12
  418.6 5.8 psum.184
  424.4 5.9 multiply_reduce_fusion.13
  431.4 3.3 fusion.84
  435.6 4.5 convolution_bitcast_fusion.3
  440.2 3.3 fusion.103
  444.6 3.9 multiply_reduce_fusion.17
  450.3 20.9 %fusion.50 = (f32[2,512,6]{1,2,0:T(8,128)S(1)}, f32[2,512,6]{1,2,0:T(8,128)S(1)}, f32[2,512,6]{1,2,0:T(8,128)}, f32[2,512,512]{2,1,0:T(8,128)}) fusion(f32[2,512,6]{1,2,0:T(8,128)S(1)} %copy-done.115, f32[2,512,512]{2,1,0:T(8,128)S(1)} %copy-done.54, f32[2,512,6]{1,2,0:T(8,128)S(1)} %copy.362, pred[512,512]{1,0:T(8,128)(4,1)S(1)} %copy-done.89, ...), kind=kOutput, calls=%fused_computation.73 | convolution fusion | flops 2462562304 | bytes 7725056 | tf_op jit(solution)/shard_map/transpose(jvp(stuh,suhp->sthp))/dot_general | solution.py:113
  476.9 13.6 %while.67 = (s32[]{:T(128)}, f32[2,512,2,64]{1,3,2,0:T(8,128)S(1)}, f32[2,4096,128]{1,2,0:T(8,128)}, s32[]{:T(128)}, bf16[2,4096,128]{1,2,0:T(8,128)(2,1)}, /*in...) while((s32[]{:T(128)}, f32[2,512,2,64]{1,3,2,0:T(8,128)S(1)}, ...), condition=%wide.region_20.21_spmd.clone, body=%wide.region_19.20_spmd.clone.sunk | while | flops 682296320 | bytes 40534276 | solution.py:367
  477.3 3.8 fusion.266
  481.3 3.9 fusion.267
  490.6 2.9 fusion.98
  493.5 4.1 convolution_add_fusion.3
  500.3 3.4 fusion.115
  503.9 4.3 rev.7
  508.1 8.3 while.69
  516.4 2.9 fusion.95
  521.8 2.7 multiply_reduce_fusion.11
  524.7 11.9 bitcast_add_fusion.3
  536.7 3.3 multiply_reduce_fusion.9
  550.3 3.0 fusion.189
  556.5 3.2 add_add_fusion.3
  561.5 16.5 %reduce-window.16 = f32[2,6,4,128]{3,2,1,0:T(4,128)} reduce-window(f32[2,6,4,128]{3,2,1,0:T(4,128)} %copy.393, f32[]{:T(128)} %constant.180.clone.1), window={size=1x1x1x128 pad=0_0x0_0x0_0x0_127}, to_apply=%region_32.33 | reduce-window | flops 780288 | bytes 49156 | tf_op jit(solution)/shard_map/reduce-window.2
  584.8 3.9 fusion.187
  589.8 3.6 fusion.176
  593.4 7.6 pad_add_fusion
  602.0 3.0 slice_add_fusion
  606.5 7.0 add_add_fusion.2
  614.1 4.7 convolution_bitcast_fusion.2
  626.6 2.8 convolution_bitcast_fusion.6
  632.4 4.1 convolution_bitcast_fusion.5
  636.5 49.5 %reduce-scatter.8.cloned.1.call-done = f32[2,512,128]{1,2,0:T(8,128)} async-done(((f32[2,4096,128]{1,2,0:T(8,128)}), f32[2,512,128]{1,2,0:T(8,128)}) %reduce-scatter.8.cloned.1.call-update) | async-done | bytes 524304 | tf_op jit(solution)/shard_map/reduce_scatter | solution.py:370
  692.2 62.3 %all-reduce.27 = (bf16[2,512,256]{1,2,0:T(8,128)(2,1)}, bf16[2,512,2,128]{3,1,2,0:T(8,128)(2,1)}, f32[4,256]{1,0:T(4,128)S(1)}) all-reduce(f32[2,512,256]{1,2,0:T(8,128)S(1)} %slice-done, f32[2,512,2,128]{3,1,2,0:T(8,128)} %broadcast_multiply_fusion.4, f32[4,256]{1,0:T(4,128)} %pad_add_fusion.3), channel_id=1, replica_groups=mesh['seq'=8,'head'=4] {'head'}, use_global_device_ids=true, to_apply=%region_37.38 | all-reduce | flops 525312 | bytes 3153920 | tf_op jit(solution)/shard_map/psum | solution.py:387
  754.5 3.1 convolution_bitcast_fusion.7
  761.1 3.9 fusion.147
  765.1 58.9 %all-reduce.24.cloned.1.call-done = f32[2,512,1024]{2,1,0:T(8,128)} async-done(((f32[2,512,1024]{2,1,0:T(8,128)}), f32[2,512,1024]{2,1,0:T(8,128)}) %all-reduce.24.cloned.1.call-update) | async-done | bytes 4194320 | tf_op jit(solution)/shard_map/psum | solution.py:387
  823.9 7.2 multiply_reduce_fusion.2
  831.2 38.3 %all-reduce.14 = (f32[1024]{0:T(1024)}, f32[1024,6]{0,1:T(8,128)}, f32[4,384]{1,0:T(4,128)}, f32[4,256]{1,0:T(4,128)}, f32[6]{0:T(128)}, /*index=5*/f32[6]{0:T(128)}, f32[6]{0:T(128)}, f32[384]{0:T(512)}, f32[1024]{0:T(1024)}) all-reduce(f32[1024]{0:T(1024)S(1)} %get-tuple-element.589, ...), channel_id=1, replica_groups=mesh['seq'=8,'head'=4] {'seq'}, use_global_device_ids=true, to_apply=%region_40.41 | all-reduce | flops 11154 | bytes 89232 | tf_op jit(solution)/shard_map/psum | solution.py:407
  869.5 7.9 fusion.64
  877.4 427.3 %all-reduce.26.cloned.1.call-done = (f32[1024,128]{1,0:T(8,128)}, f32[1024,2,128]{2,0,1:T(8,128)}, f32[128,1024]{1,0:T(8,128)}, f32[1024,384]{1,0:T(8,128)}, f32...) async-done(((f32[1024,128]{1,0:T(8,128)}, ...) | async-done | bytes 14155792 | tf_op jit(solution)/shard_map/psum | solution.py:407
  1304.8 3.0 copy.417
  (491 shorter events, 181.3 us)
Async XLA Ops:
  7.2 306.1 %copy-start = (bf16[512,1024]{1,0:T(8,128)(2,1)S(1)}, bf16[512,1024]{1,0:T(8,128)(2,1)}, u32[]{:S(2)}) copy-start(bf16[512,1024]{1,0:T(8,128)(2,1)} %param.50) | copy-start | bytes 3145732
  7.2 6.7 copy-start.9
  7.2 94.7 %all-gather.9.cloned.1.call-start = ((), (), s32[]{:S(2)}) async-start(), calls=%async_computation.3 | async-start | bytes 2359296 | tf_op jit(solution)/shard_map/all_gather | solution.py:188
  11.8 182.1 %copy-start.97 = (f32[1024]{0:T(1024)}, f32[1024]{0:T(1024)S(1)}, u32[]{:S(2)}) copy-start(f32[1024]{0:T(1024)S(1)} %convert_element_type.100) | copy-start | bytes 12292
  13.9 180.0 %copy-start.99 = (f32[2,512]{1,0:T(2,128)}, f32[2,512]{1,0:T(2,128)S(1)}, u32[]{:S(2)}) copy-start(f32[2,512]{1,0:T(2,128)S(1)} %fusion.180) | copy-start | bytes 12292
  18.4 141.3 %all-gather.15.cloned.1.call-start = ((), (), s32[]{:S(2)}) async-start(), calls=%async_computation.11 | async-start | bytes 3538944 | tf_op jit(solution)/shard_map/all_gather | solution.py:28
  24.0 11.4 copy-start.141
  24.0 11.4 copy-start.131
  25.9 31.3 %copy-start.87 = (bf16[1024,128]{1,0:T(8,128)(2,1)S(1)}, bf16[1024,128]{1,0:T(8,128)(2,1)}, u32[]{:S(2)}) copy-start(bf16[1024,128]{1,0:T(8,128)(2,1)} %param.33) | copy-start | bytes 786436
  25.9 59.1 %collective-permute-start = (f32[2,3,640]{2,0,1:T(2,128)}, f32[2,3,640]{2,0,1:T(2,128)}, u32[]{:S(2)}, u32[]{:S(2)}) collective-permute-start(f32[2,3,640]{2,0,1:T(2,128)} %copy.353), channel_id=1, source_target_pairs={{0,4},{4,8},{8,12},{12,16},{16,20},{20,24},{24,28},{1,5},{5,9},{9,... | collective-permute-start | bytes 46088 | tf_op jit(solution)/shard_map/ppermute | solution.py:23
  58.2 8.5 copy-start.137
  61.0 28.7 %copy-start.101 = (f32[640]{0:T(1024)}, f32[640]{0:T(1024)S(1)}, u32[]{:S(2)}) copy-start(f32[640]{0:T(1024)S(1)} %get-tuple-element.597) | copy-start | bytes 7684
  61.1 28.7 %copy-start.103 = (f32[640]{0:T(1024)}, f32[640]{0:T(1024)S(1)}, u32[]{:S(2)}) copy-start(f32[640]{0:T(1024)S(1)} %get-tuple-element.598) | copy-start | bytes 7684
  61.1 28.7 %copy-start.105 = (f32[640]{0:T(1024)}, f32[640]{0:T(1024)S(1)}, u32[]{:S(2)}) copy-start(f32[640]{0:T(1024)S(1)} %get-tuple-element.599) | copy-start | bytes 7684
  61.1 28.7 %copy-start.107 = (f32[640]{0:T(1024)}, f32[640]{0:T(1024)S(1)}, u32[]{:S(2)}) copy-start(f32[640]{0:T(1024)S(1)} %get-tuple-element.600) | copy-start | bytes 7684
  62.3 388.0 %copy-start.113 = (f32[2,512,6]{1,2,0:T(8,128)}, f32[2,512,6]{1,2,0:T(8,128)S(1)}, u32[]{:S(2)}) copy-start(f32[2,512,6]{1,2,0:T(8,128)S(1)} %copy.362) | copy-start | bytes 73732
  63.6 29.8 %copy-start.84 = (f32[2,512,6]{1,2,0:T(8,128)}, f32[2,512,6]{1,2,0:T(8,128)S(1)}, u32[]{:S(2)}) copy-start(f32[2,512,6]{1,2,0:T(8,128)S(1)} %copy.369) | copy-start | bytes 73732
  66.7 363.6 %copy-start.86 = (f32[2,512,6]{1,2,0:T(8,128)}, f32[2,512,6]{1,2,0:T(8,128)S(1)}, u32[]{:S(2)}) copy-start(f32[2,512,6]{1,2,0:T(8,128)S(1)} %copy.367) | copy-start | bytes 73732
  101.9 166.1 %reduce-scatter.4.cloned.1.call-start = ((), (), s32[]{:S(2)}) async-start(), calls=%async_computation.4 | async-start | bytes 5242880 | tf_op jit(solution)/shard_map/reduce_scatter | solution.py:259
  159.7 16.4 %copy-start.139 = (f32[6]{0:T(128)S(1)}, f32[6]{0:T(128)}, u32[]{:S(2)}) copy-start(f32[6]{0:T(128)} %param.44) | copy-start | bytes 76
  176.1 17.8 %copy-start.44 = (f32[2,512,6,64]{1,3,2,0:T(8,128)}, f32[2,512,6,64]{1,3,2,0:T(8,128)S(1)}, u32[]{:S(2)}) copy-start(f32[2,512,6,64]{1,3,2,0:T(8,128)S(1)} %fusion.137) | copy-start | bytes 4718596
  176.1 17.8 %copy-start.76 = (bf16[1024,384]{1,0:T(8,128)(2,1)S(1)}, bf16[1024,384]{1,0:T(8,128)(2,1)}, u32[]{:S(2)}) copy-start(bf16[1024,384]{1,0:T(8,128)(2,1)} %param.36) | copy-start | bytes 2359300
  209.1 96.3 %all-gather.11.cloned.1.call-start = ((), (), s32[]{:S(2)}) async-start(), calls=%async_computation.5 | async-start | bytes 5242880 | tf_op jit(solution)/shard_map/all_gather | solution.py:263
  211.6 59.4 %copy-start.133 = (bf16[1024]{0:T(1024)(128)(2,1)S(1)}, bf16[1024]{0:T(1024)(128)(2,1)}, u32[]{:S(2)}) copy-start(bf16[1024]{0:T(1024)(128)(2,1)} %param.47) | copy-start | bytes 6148
  270.7 136.3 %all-reduce.22.cloned.1.call-start = ((), (), s32[]{:S(2)}) async-start(), calls=%async_computation.8 | async-start | bytes 8388608 | tf_op jit(solution)/shard_map/psum | solution.py:281
  270.9 141.4 %copy-start.91 = (f32[1024]{0:T(1024)}, f32[1024]{0:T(1024)S(1)}, u32[]{:S(2)}) copy-start(f32[1024]{0:T(1024)S(1)} %convert_element_type.107) | copy-start | bytes 12292
  308.8 103.5 %copy-start.93 = (f32[2,512]{1,0:T(2,128)}, f32[2,512]{1,0:T(2,128)S(1)}, u32[]{:S(2)}) copy-start(f32[2,512]{1,0:T(2,128)S(1)} %fusion.181) | copy-start | bytes 12292
  321.4 182.5 %all-gather.17.cloned.1.call-start = ((), (), s32[]{:S(2)}) async-start(), calls=%async_computation.12 | async-start | bytes 3538944 | tf_op jit(solution)/shard_map/all_gather | solution.py:28
  407.0 5.9 copy-start.8
  434.8 194.7 %reduce-scatter.6.cloned.1.call-start = ((), (), s32[]{:S(2)}) async-start(), calls=%async_computation.6 | async-start | bytes 5242880 | tf_op jit(solution)/shard_map/reduce_scatter | solution.py:270
  443.5 242.5 %reduce-scatter.8.cloned.1.call-start = ((), (), s32[]{:S(2)}) async-start(), calls=%async_computation.10 | async-start | bytes 4718592 | tf_op jit(solution)/shard_map/reduce_scatter | solution.py:370
  444.6 5.7 copy-start.12
  444.6 5.7 copy-start.54
  444.6 5.7 copy-start.89
  444.6 5.7 copy-start.115
  476.9 13.6 %copy-start.78 = (f32[512,32]{0,1:T(8,128)S(1)}, f32[512,32]{0,1:T(8,128)}, u32[]{:S(2)}) copy-start(f32[512,32]{0,1:T(8,128)} %get-tuple-element.737) | copy-start | bytes 196612
  476.9 13.6 %copy-start.79 = (f32[512,32]{0,1:T(8,128)S(1)}, f32[512,32]{0,1:T(8,128)}, u32[]{:S(2)}) copy-start(f32[512,32]{0,1:T(8,128)} %get-tuple-element.738) | copy-start | bytes 196612
  490.6 7.0 copy-start.88
  503.8 320.1 %all-reduce.24.cloned.1.call-start = ((), (), s32[]{:S(2)}) async-start(), calls=%async_computation.9 | async-start | bytes 8388608 | tf_op jit(solution)/shard_map/psum | solution.py:387
  508.1 8.3 copy-start.85
  524.6 12.0 copy-start.3
  524.6 12.0 copy-start.21
  524.6 12.0 copy-start.34
  524.6 12.0 copy-start.37
  524.6 12.0 copy-start.62
  544.8 5.5 copy-start.129
  546.0 8.5 copy-start.117
  546.0 9.6 copy-start.17
  548.0 53.1 %collective-permute-start.1 = (f32[2,3,640]{2,0,1:T(2,128)}, f32[2,3,640]{2,0,1:T(2,128)}, u32[]{:S(2)}, u32[]{:S(2)}) collective-permute-start(f32[2,3,640]{2,0,1:T(2,128)} %copy.385), channel_id=1, source_target_pairs={{4,0},{8,4},{12,8},{16,12},{20,16},{24,20},{28,24},{5,1},{9,5},{13... | collective-permute-start | bytes 46088 | tf_op jit(solution)/shard_map/ppermute | solution.py:23
  555.7 29.1 %copy-start.42 = (f32[2,512,6]{2,0,1:T(2,128)S(1)}, f32[2,512,6]{2,0,1:T(2,128)}, u32[]{:S(2)}) copy-start(f32[2,512,6]{2,0,1:T(2,128)} %copy.355) | copy-start | bytes 73732
  555.7 29.1 %copy-start.43 = (f32[2,512,6]{2,0,1:T(2,128)S(1)}, f32[2,512,6]{2,0,1:T(2,128)}, u32[]{:S(2)}) copy-start(f32[2,512,6]{2,0,1:T(2,128)} %get-tuple-element.701) | copy-start | bytes 73732
  589.8 11.3 copy-start.95
  613.6 263.9 %all-gather.13.cloned.1.call-start = ((), (), s32[]{:S(2)}) async-start(), calls=%async_computation.7 | async-start | bytes 2621440 | tf_op jit(solution)/shard_map/all_gather | solution.py:272
  631.7 673.1 %all-reduce.26.cloned.1.call-start = ((), (), s32[]{:S(2)}) async-start(), calls=%async_computation.13 | async-start | bytes 28311552 | tf_op jit(solution)/shard_map/psum | solution.py:407
  761.1 62.8 %copy-start.56 = (bf16[1024,2,128]{2,1,0:T(2,128)(2,1)S(1)}, bf16[1024,2,128]{2,1,0:T(2,128)(2,1)}, u32[]{:S(2)}) copy-start(bf16[1024,2,128]{2,1,0:T(2,128)(2,1)} %param.34) | copy-start | bytes 1572868
  765.0 66.1 %copy-start.123 = (f32[1024]{0:T(1024)S(1)}, f32[1024]{0:T(1024)}, u32[]{:S(2)}) copy-start(f32[1024]{0:T(1024)} %get-tuple-element.587) | copy-start | bytes 12292
  765.0 66.1 %copy-start.134 = (f32[384]{0:T(512)S(1)}, f32[384]{0:T(512)}, u32[]{:S(2)}) copy-start(f32[384]{0:T(512)} %get-tuple-element.594) | copy-start | bytes 4612
  765.0 66.1 %copy-start.136 = (f32[6]{0:T(128)S(1)}, f32[6]{0:T(128)}, u32[]{:S(2)}) copy-start(f32[6]{0:T(128)} %get-tuple-element.693) | copy-start | bytes 76
  765.0 104.5 %copy-start.110 = (f32[2,512]{1,0:T(2,128)S(1)}, f32[2,512]{1,0:T(2,128)}, u32[]{:S(2)}) copy-start(f32[2,512]{1,0:T(2,128)} %copy-done.109) | copy-start | bytes 12292
  765.0 104.5 %copy-start.92 = (f32[1024]{0:T(1024)S(1)}, f32[1024]{0:T(1024)}, u32[]{:S(2)}) copy-start(f32[1024]{0:T(1024)} %copy-done.91) | copy-start | bytes 12292
  765.0 104.5 %copy-start.94 = (f32[2,512]{1,0:T(2,128)S(1)}, f32[2,512]{1,0:T(2,128)}, u32[]{:S(2)}) copy-start(f32[2,512]{1,0:T(2,128)} %copy-done.93) | copy-start | bytes 12292
  765.0 104.5 %copy-start.112 = (f32[2,512]{1,0:T(2,128)S(1)}, f32[2,512]{1,0:T(2,128)}, u32[]{:S(2)}) copy-start(f32[2,512]{1,0:T(2,128)} %copy-done.111) | copy-start | bytes 12292
  823.9 7.2 slice-start.1
  877.4 430.3 %copy-start.58 = (bf16[2,512,1024]{2,1,0:T(8,128)(2,1)S(1)}, bf16[2,512,1024]{2,1,0:T(8,128)(2,1)}, u32[]{:S(2)}) copy-start(bf16[2,512,1024]{2,1,0:T(8,128)(2,1)} %all-gather.13.cloned.1.call-done) | copy-start | bytes 6291460
  (94 other events, 242.0 us)
Sparse Core Ops, SparseCore 0:
  18.6 53.7 all-gather.8
  102.0 57.6 all-gather.14
  209.2 58.7 reduce-scatter.3
  270.8 34.4 all-gather.10
  321.5 85.4 all-reduce.21
  434.9 61.0 all-gather.16
  499.1 43.0 reduce-scatter.5
  546.3 139.6 reduce-scatter.7
  688.4 135.4 all-reduce.23
  826.0 22.7 all-gather.12
  858.0 446.7 all-reduce.25
where the time goes:
time: 1340 us; the launch traced here: 1330 us
  waiting for transfers between devices  754 us (56%)
  matrix products  194 us (14%)
  other arithmetic  141 us (11%)
  blocking collectives  130 us (10%)
  local copies, waits for them, and re-layouts  83.6 us (6%)
  between operations  15.7 us (1%)
    psum x1, waiting for transfers between devices, on_device(): lax.psum((grad_gain_one, grad_query, grad_keyvalue, grad_output_proj, gra...  427 us
    psum x1, waiting for transfers between devices, on_device(): lax.psum(matmul_back(gate_grad, gate_weight) + matmul_back(up_grad, up_we...  85.6 us
    psum x1, blocking collectives, on_device(): lax.psum((normed_part, keyvalue_both, inner_grad[..., inner_width:], conv...  62.3 us
    psum x1, waiting for transfers between devices, on_device(): lax.psum((normed_part, keyvalue_both, inner_grad[..., inner_width:], conv...  58.9 us
    reduce_scatter x1, waiting for transfers between devices, on_device(): lax.psum_scatter(branch_part, 'head', scatter_dimension=1, tiled=True)  56.4 us
    dot_general x3, matrix products, intra(): jnp.einsum('stuh,suhp->sthp', mixing, channels, precision=HIGH_ACCURACY)  50.6 us
    reduce_scatter x1, waiting for transfers between devices, on_device(): lax.psum_scatter(keyvalue_grad_all, 'seq', scatter_dimension=1, tiled=True)  49.5 us
    all_gather x2, waiting for transfers between devices, prefix(): pieces = jax.tree.map(lambda part: lax.all_gather(part, axis), value)  42 us
  transfers between devices with their start and end apart: 13, of which 7 were waited for; matrix products, arithmetic and copies ran while one was open for 22% of the time, Pallas kernels for 0%

commit v1 on v0

--- a/solution.py
+++ b/solution.py
@@ -23,21 +23,41 @@
     return lax.ppermute(value, axis, [(source, source + steps) for source in range(first, last)])
 
 
-def prefix(value, axis, join, neutral, backward):
+def carried(log_totals, states, axis, backward):
     count, mine = (lax.axis_size(axis), lax.axis_index(axis))
-    pieces = jax.tree.map(lambda part: lax.all_gather(part, axis), value)
+    pieces = lax.all_gather(states.astype(jnp.bfloat16), axis)
+    place = jnp.arange(count, dtype=jnp.int32)
     if backward:
-        pieces = jax.tree.map(lambda part: part[::-1], pieces)
-        mine = count - 1 - mine
-    running = jax.tree.map(
-        lambda part, zero: jnp.full_like(part, 0) + jnp.asarray(zero, part.dtype), value, neutral
-    )
-
-    def step(position, running):
-        longer = join(running, jax.tree.map(lambda part: part[position], pieces))
-        return jax.tree.map(lambda new, old: jnp.where(position < mine, new, old), longer, running)
-
-    return lax.fori_loop(0, count - 1, step, running)
+        between = (place[None, :] < place[:, None]) & (place[None, :] > mine)
+        used = place > mine
+    else:
+        between = (place[None, :] > place[:, None]) & (place[None, :] < mine)
+        used = place < mine
+    decay = jnp.sum(
+        jnp.where(between[:, :, None, None], log_totals[None], 0.0), axis=1
+    )
+    weight = jnp.where(used[:, None, None], jnp.exp(decay), 0.0)
+    return jnp.sum(weight[..., None, None] * pieces.astype(jnp.float32), axis=0)
+
+
+def summed_share(value, axis):
+    count = lax.axis_size(axis)
+    pieces = value.astype(jnp.bfloat16).reshape(count, value.shape[0] // count, *value.shape[1:])
+    landed = lax.all_to_all(pieces, axis, 0, 0)
+    return jnp.sum(landed.astype(jnp.float32), axis=0)
+
+
+def summed_rows(value, axis):
+    count = lax.axis_size(axis)
+    sequences, rows, width = value.shape
+    pieces = value.astype(jnp.bfloat16).reshape(sequences, count, rows // count, width)
+    landed = lax.all_to_all(pieces, axis, 1, 1)
+    return jnp.sum(landed.astype(jnp.float32), axis=1)
+
+
+def summed_everywhere(value, axis):
+    share = summed_share(value, axis).astype(jnp.bfloat16)
+    return lax.all_gather(share, axis, axis=0, tiled=True).astype(jnp.float32)
 
 
 def matmul(left_operand, right_operand):
@@ -126,15 +146,19 @@
     channels, writes, reads, step, logdecay = ssm_inputs(
         extended, step_raw, conv_weight, step_bias, decay_log
     )
-    running = jnp.cumsum(logdecay, axis=1)
+    running = running_sum(logdecay)
     within, local = intra(channels, writes, reads, step, running)
     result = within + inter(reads, running, state_in) + skip_gain[:, None] * channels
     state_end = jnp.exp(running[:, -1])[:, :, None, None] * state_in + local
     return (result, state_end)
 
 
-def chain(earlier, later):
-    return (earlier[0] * later[0], later[0][:, :, None, None] * earlier[1] + later[1])
+def running_sum(values):
+    rows = values.shape[1]
+    lower = jnp.arange(rows, dtype=jnp.int32)[:, None] >= jnp.arange(rows, dtype=jnp.int32)[None, :]
+    return jnp.einsum(
+        "tu,suh->sth", lower.astype(jnp.float32), values, precision=HIGH_ACCURACY
+    )
 
 
 def on_device(
@@ -242,11 +266,10 @@
     channels, writes, reads, step, logdecay = ssm_inputs(
         extended, step_raw, conv_weight, step_bias, decay_log
     )
-    running = jnp.cumsum(logdecay, axis=1)
+    running = running_sum(logdecay)
     within, local = intra(channels, writes, reads, step, running)
-    decay_all = jnp.exp(running[:, -1])
-    identity = (jnp.ones_like(decay_all), jnp.zeros_like(local))
-    state_in = prefix((decay_all, local), "seq", chain, identity, False)[1]
+    log_totals = lax.all_gather(running[:, -1], "seq")
+    state_in = carried(log_totals, local, "seq", False)
     y_ssm = within + inter(reads, running, state_in) + skip_gain[:, None] * channels
     y_flat = y_ssm.reshape(sequences, rows, inner_width)
     gated = y_flat * jax.nn.silu(zgate)
@@ -256,18 +279,20 @@
     ssm_normed = (gated * ssm_factor * gain_ssm).astype(jnp.bfloat16)
     branch_part = matmul(attended, output_weight) + matmul(ssm_normed, mixer_weight)
     quarter = rows // lax.axis_size("head")
-    mixed_rows = lax.psum_scatter(branch_part, "head", scatter_dimension=1, tiled=True)
-    hidden_rows = (
-        lax.dynamic_slice_in_dim(input_float, head_index * quarter, quarter, 1) + mixed_rows
-    )
-    hidden = lax.all_gather(hidden_rows, "head", axis=1, tiled=True)
+    mixed_rows = summed_rows(branch_part, "head")
+    def own_rows(value):
+        return lax.dynamic_slice_in_dim(value, head_index * quarter, quarter, 1)
+
+    input_rows = own_rows(input_float)
+    hidden_rows = input_rows + mixed_rows
     gain_two = mlp_gain.astype(jnp.float32)
-    normed_two = rms_norm(hidden, gain_two).astype(jnp.bfloat16)
+    normed_two_rows = rms_norm(hidden_rows, gain_two).astype(jnp.bfloat16)
+    normed_two = lax.all_gather(normed_two_rows, "head", axis=1, tiled=True)
     gate = matmul(normed_two, gate_weight)
     up = matmul(normed_two, up_weight)
     activated = (jax.nn.silu(gate) * up).astype(jnp.bfloat16)
     feed_part = matmul(activated, down_weight)
-    feed_own = lax.psum_scatter(feed_part, "head", scatter_dimension=1, tiled=True)
+    feed_own = summed_rows(feed_part, "head")
     output_own = (hidden_rows + feed_own).astype(jnp.bfloat16)
     output = lax.all_gather(output_own, "head", axis=1, tiled=True)
     act_grad = matmul_back(grad_output, down_weight)
@@ -278,13 +303,18 @@
     up_grad = up_grad.astype(jnp.bfloat16)
     grad_gate = weight_grad(normed_two, gate_grad)
     grad_up = weight_grad(normed_two, up_grad)
-    normed_two_grad = lax.psum(
+    normed_two_grad = summed_rows(
         matmul_back(gate_grad, gate_weight) + matmul_back(up_grad, up_weight), "head"
     )
-    norm_two_pull = jax.vjp(rms_norm, hidden, gain_two)[1]
+    units = grad_down.shape[0]
+    down_sum = summed_everywhere(grad_down, "seq")
+    feed_sums = summed_everywhere(jnp.concatenate([grad_gate, grad_up], axis=1), "seq")
+    norm_two_pull = jax.vjp(rms_norm, hidden_rows, gain_two)[1]
     hidden_norm_grad, grad_gain_two = norm_two_pull(normed_two_grad)
-    hidden_grad = grad_output.astype(jnp.float32) + hidden_norm_grad
-    mixed_grad = hidden_grad.astype(jnp.bfloat16)
+    hidden_grad = own_rows(grad_output).astype(jnp.float32) + hidden_norm_grad
+    mixed_grad = lax.all_gather(
+        hidden_grad.astype(jnp.bfloat16), "head", axis=1, tiled=True
+    )
     grad_output_proj = weight_grad(attended, mixed_grad)
     attended_grad = (
         matmul_back(mixed_grad, output_weight)
@@ -292,6 +322,7 @@
         .reshape(sequences, rows, heads_here, head_dim)
     )
     grad_mixer = weight_grad(ssm_normed, mixed_grad)
+    mixed_sums = summed_everywhere(jnp.concatenate([grad_output_proj, grad_mixer], axis=0), "seq")
     ssm_normed_grad = matmul_back(mixed_grad, mixer_weight)
     weighted = ssm_normed_grad * gain_ssm
     inner_total = lax.psum(jnp.sum(weighted * gated, axis=-1), "head")
@@ -305,7 +336,7 @@
     own_state_grad = jnp.einsum(
         "sth,stn,sthp->shpn", jnp.exp(running), reads, y_grad_heads, precision=HIGH_ACCURACY
     )
-    state_grad = prefix((decay_all, own_state_grad), "seq", chain, identity, True)[1]
+    state_grad = carried(log_totals, own_state_grad, "seq", True)
     ssm_pull = jax.vjp(
         ssm_full, extended, step_raw, conv_weight, step_bias, decay_log, skip_gain, state_in
     )[1]
@@ -367,7 +398,7 @@
     query_grad, keyvalue_grad_all = lax.fori_loop(
         0, blocks_needed, make_back_pass(), (query_zero, keyvalue_zero)
     )
-    keyvalue_grad_own = lax.psum_scatter(keyvalue_grad_all, "seq", scatter_dimension=1, tiled=True)
+    keyvalue_grad_own = summed_rows(keyvalue_grad_all, "seq")
     key_raw_grad = rotate(keyvalue_grad_own[:, :, None, :head_dim], -positions)[:, :, 0]
     keyvalue_raw_grad = jnp.concatenate([key_raw_grad, keyvalue_grad_own[..., head_dim:]], axis=-1)
     chooser = (jnp.arange(KV_HEADS, dtype=jnp.int32) == kv_index).astype(jnp.float32)
@@ -384,51 +415,85 @@
         + matmul_back(inner_own, inner_weight)
         + matmul_back(step_grad, step_weight)
     )
-    normed_sum, keyvalue_sum, state_sum, conv_state_grad = lax.psum(
-        (normed_part, keyvalue_both, inner_grad[..., inner_width:], conv_grad[:, inner_width:]),
+    kv_width = keyvalue_both.shape[2] * keyvalue_both.shape[3]
+    together = summed_rows(
+        jnp.concatenate(
+            [
+                normed_part,
+                keyvalue_both.reshape(sequences, rows, kv_width),
+                inner_grad[..., inner_width:],
+            ],
+            axis=-1,
+        ),
         "head",
     )
-    keyvalue_low = keyvalue_sum.astype(jnp.bfloat16)
-    state_low = state_sum.astype(jnp.bfloat16)
-    grad_keyvalue = jnp.einsum(
-        "std,sthe->dhe", normalized_input, keyvalue_low, preferred_element_type=jnp.float32
-    )
-    grad_state = weight_grad(normalized_input, state_low)
-    normed_grad = (
-        normed_sum
-        + jnp.einsum(
-            "sthe,dhe->std", keyvalue_low, keyvalue_matrix, preferred_element_type=jnp.float32
-        )
-        + matmul_back(state_low, state_weight)
-    )
-    norm_one_pull = jax.vjp(rms_norm, input_float, gain_one)[1]
+    normed_sum = together[..., :width]
+    low_rows = together[..., width:].astype(jnp.bfloat16)
+    shared_weight = jnp.concatenate(
+        [keyvalue_matrix.reshape(width, kv_width), state_weight], axis=1
+    )
+    grad_shared = weight_grad(own_rows(normalized_input), low_rows)
+    normed_grad = normed_sum + matmul_back(low_rows, shared_weight)
+    norm_one_pull = jax.vjp(rms_norm, input_rows, gain_one)[1]
     input_norm_grad, grad_gain_one = norm_one_pull(normed_grad)
-    grad_input = hidden_grad + input_norm_grad
-    summed_grads = lax.psum(
-        (
-            grad_gain_one,
-            grad_query,
-            grad_keyvalue,
-            grad_output_proj,
-            grad_zgate,
-            grad_inner,
-            grad_state,
-            grad_step,
-            conv_grad[:, :inner_width],
-            conv_state_grad,
-            grad_step_bias,
-            grad_decay_log,
-            grad_skip,
-            grad_gain_ssm,
-            grad_mixer,
-            grad_gain_two,
-            grad_gate,
-            grad_up,
-            grad_down,
-        ),
-        "seq",
-    )
-    return (output, grad_input) + tuple(summed_grads)
+    input_rows_grad = (hidden_grad + input_norm_grad).astype(jnp.bfloat16)
+    grad_input = lax.all_gather(input_rows_grad, "head", axis=1, tiled=True).astype(jnp.float32)
+    last_sums = summed_everywhere(
+        jnp.concatenate([grad_zgate, grad_inner, grad_query], axis=1), "seq"
+    )
+    shared_part = summed_share(summed_share(grad_shared, "head"), "seq").astype(jnp.bfloat16)
+    shared_sum = lax.all_gather(
+        shared_part, ("head", "seq"), axis=0, tiled=True
+    ).astype(jnp.float32)
+    own_small = [
+        grad_step,
+        conv_grad[:, :inner_width],
+        grad_step_bias,
+        grad_decay_log,
+        grad_skip,
+        grad_gain_ssm,
+    ]
+    all_small = [grad_gain_one, grad_gain_two, conv_grad[:, inner_width:]]
+
+    def unpacked(flat, likes):
+        found, at = [], 0
+        for like in likes:
+            found.append(flat[at : at + like.size].reshape(like.shape))
+            at += like.size
+        return found
+
+    own_flat = lax.psum(jnp.concatenate([part.reshape(-1) for part in own_small]), "seq")
+    all_flat = lax.psum(
+        jnp.concatenate([part.reshape(-1) for part in all_small]), ("seq", "head")
+    )
+    grad_step, conv_inner_grad, grad_step_bias, grad_decay_log, grad_skip, grad_gain_ssm = unpacked(
+        own_flat, own_small
+    )
+    grad_gain_one, grad_gain_two, conv_state_grad = unpacked(all_flat, all_small)
+    attended_width = heads_here * head_dim
+    return (
+        output,
+        grad_input,
+        grad_gain_one,
+        last_sums[:, 2 * inner_width :],
+        shared_sum[:, :kv_width].reshape(keyvalue_matrix.shape),
+        mixed_sums[:attended_width],
+        last_sums[:, :inner_width],
+        last_sums[:, inner_width : 2 * inner_width],
+        shared_sum[:, kv_width:],
+        grad_step,
+        conv_inner_grad,
+        conv_state_grad,
+        grad_step_bias,
+        grad_decay_log,
+        grad_skip,
+        grad_gain_ssm,
+        mixed_sums[attended_width:],
+        grad_gain_two,
+        feed_sums[:, :units],
+        feed_sums[:, units:],
+        down_sum,
+    )
 
 
 def solution(mesh):

time: 1340 us -> 925 us (0.69)
  waiting for transfers between devices: 754 us -> 273 us
  starting transfers between devices: 8.18 us -> 136 us
  other arithmetic: 141 us -> 95.6 us
  blocking collectives: 130 us -> 170 us
  matrix products: 194 us -> 156 us
  local copies, waits for them, and re-layouts: 83.6 us -> 66.9 us
    psum x3 -> x0, waiting for transfers between devices: 572 us -> none  [the longest x1 427 us: on_device(): lax.psum((grad_gain_one, grad_query, grad_keyvalue, grad_output_proj, gra...]
    all_to_all x0 -> x8, waiting for transfers between devices: none -> 173 us  [the longest x4 108 us: summed_share(): landed = lax.all_to_all(pieces, axis, 0, 0)]
    all_to_all x0 -> x8, starting transfers between devices: none -> 128 us  [the longest x4 105 us: summed_rows(): landed = lax.all_to_all(pieces, axis, 1, 1)]
    reduce_scatter x3 -> x0, waiting for transfers between devices: 106 us -> none  [the longest x1 56.4 us: on_device(): lax.psum_scatter(branch_part, 'head', scatter_dimension=1, tiled=True)]
    all_to_all x0 -> x3, blocking collectives: none -> 64.9 us  [the longest x2 36.8 us: summed_share(): landed = lax.all_to_all(pieces, axis, 0, 0)]
    psum x2, blocking collectives: 101 us -> 72.5 us  [the longest x1 37 us: on_device(): lax.psum(jnp.concatenate([part.reshape(-1) for part in all_small]), ('seq...]
    another operation x9 -> x3, other arithmetic: 28.2 us -> 3.8 us
    all_gather x1, waiting for transfers between devices: 0.02 us -> 22.2 us  [on_device(): keyvalue_all = lax.all_gather(keyvalue_own, 'seq', axis=1, tiled=True)]
  transfers between devices with their start and end apart: 13 -> 22, of which waited for: 7 -> 10; matrix products, arithmetic and copies ran while one was open for 22% -> 28% of each run, Pallas kernels for 0% -> 0%
where the time goes in v1:
time: 925 us; the launch traced here: 914 us
  waiting for transfers between devices  273 us (30%)
  blocking collectives  170 us (18%)
  matrix products  156 us (17%)
  starting transfers between devices  136 us (15%)
  other arithmetic  95.6 us (10%)
  local copies, waits for them, and re-layouts  66.9 us (7%)
  between operations  16.5 us (2%)
    all_to_all x4, waiting for transfers between devices, summed_share(): landed = lax.all_to_all(pieces, axis, 0, 0)  108 us
    all_to_all x4, starting transfers between devices, summed_rows(): landed = lax.all_to_all(pieces, axis, 1, 1)  105 us
    all_to_all x4, waiting for transfers between devices, summed_rows(): landed = lax.all_to_all(pieces, axis, 1, 1)  64.6 us
    all_gather x1, waiting for transfers between devices, on_device(): normed_two = lax.all_gather(normed_two_rows, 'head', axis=1, tiled=True)  61.3 us
    dot_general x3, matrix products, intra(): jnp.einsum('stuh,suhp->sthp', mixing, channels, precision=HIGH_ACCURACY)  50.2 us
    psum x1, blocking collectives, on_device(): lax.psum(jnp.concatenate([part.reshape(-1) for part in all_small]), ('seq...  37 us
    all_to_all x2, blocking collectives, summed_share(): landed = lax.all_to_all(pieces, axis, 0, 0)  36.8 us
    psum x1, blocking collectives, on_device(): lax.psum(jnp.concatenate([part.reshape(-1) for part in own_small]), 'seq')  35.6 us
  transfers between devices with their start and end apart: 22, of which 10 were waited for; matrix products, arithmetic and copies ran while one was open for 28% of the time, Pallas kernels for 0%

profile of v1, /device:TPU:0, one launch (start us, length us, event | category | flops | bytes accessed | tf_op | source)
XLA Modules:
  0.0 913.7 jit_solution(2334259005817332331)
XLA Ops:
  17.3 4.9 collective-permute-start
  26.0 2.9 maximum_maximum_fusion
  29.0 3.3 fusion.66
  47.8 20.6 %all-gather = f32[16,1,6]{2,1,0:T(1,128)S(1)} all-gather(f32[2,1,6]{2,1,0:T(1,128)S(1)} %copy.251), channel_id=2, replica_groups=mesh['seq'=8,'head'=4] {'seq'}, dimensions={0}, use_global_device_ids=true | all-gather | bytes 432 | tf_op jit(solution)/shard_map/all_gather | solution.py:271
  74.9 4.4 fusion.157
  87.0 15.5 %fusion.77 = f32[2,512,6,64]{1,3,2,0:T(8,128)S(1)} fusion(f32[2,512,6,64]{1,3,2,0:T(8,128)S(1)} %bitcast.406, f32[2,512,6,64]{1,3,2,0:T(8,128)S(1)} %fusion.149, f32[2,512,6]{1,2,0:T(8,128)S(1)} %copy-done.114, f32[2,512,512]{2,1,0:T(8,128)S(1)} %copy-done.55, f32[2,512,6]{1,2,0:T(8,128)S(1)} %copy-done.93, pred[512,512]{1,0:T(8,128)(4,1)S(1)} %copy-done.90, ...), kind=kOutput, calls=%fused_computation.142 | convolution fusion | flops 2433220608 | bytes 7151640 | tf_op jit(solution)/shard_map/stuh,suhp->sthp/dot_general | solution.py:133
  102.6 2.9 multiply_reduce_fusion.11
  105.5 5.9 psum.28
  112.0 22.2 %all-gather.16.cloned.1.call-done = bf16[2,4096,128]{1,2,0:T(8,128)(2,1)} async-done(((bf16[2,512,128]{1,2,0:T(8,128)(2,1)}), bf16[2,4096,128]{1,2,0:T(8,128)(2,1)}) %all-gather.16.cloned.1.call-update) | async-done | bytes 2097168 | tf_op jit(solution)/shard_map/all_gather | solution.py:212
  134.3 3.0 while.37
  137.4 2.9 while.38
  145.2 4.6 all-to-all-start
  152.6 23.0 %all-to-all-done = bf16[2,4,128,1024]{3,2,0,1:T(8,128)(2,1)} async-done(((bf16[2,4,128,1024]{3,2,0,1:T(8,128)(2,1)}), bf16[2,4,128,1024]{3,2,0,1:T(8,128)(2,1)}, u32[]{:S(2)}, u32[]{:S(2)}) %all-to-all-start) | async-done | bytes 2097184 | tf_op jit(solution)/shard_map/all_to_all | solution.py:54
  181.1 61.3 %all-gather.18.cloned.1.call-done = bf16[2,512,1024]{2,1,0:T(8,128)(2,1)} async-done(((bf16[2,128,1024]{2,1,0:T(8,128)(2,1)}), bf16[2,512,1024]{2,1,0:T(8,128)(2,1)}) %all-gather.18.cloned.1.call-update) | async-done | bytes 2097168 | tf_op jit(solution)/shard_map/all_gather | solution.py:290
  242.4 3.2 fusion.119
  247.2 3.1 multiply_convert_fusion.1
  253.8 28.2 %all_to_all.55 = bf16[2,4,128,1024]{3,2,0,1:T(8,128)(2,1)S(1)} all-to-all(bf16[2,4,128,1024]{3,2,0,1:T(8,128)(2,1)S(1)} %copy.260), channel_id=1, replica_groups=mesh['seq'=8,'head'=4] {'head'}, dimensions={1} | all-to-all | bytes 4194304 | tf_op jit(solution)/shard_map/all_to_all | solution.py:54
  285.4 3.8 bitcast_convert_fusion
  289.2 5.6 all-to-all-start.10
  294.9 13.2 %all-gather.22.cloned.1.call-done = bf16[2,512,1024]{2,1,0:T(8,128)(2,1)} async-done(((bf16[2,128,1024]{2,1,0:T(8,128)(2,1)}), bf16[2,512,1024]{2,1,0:T(8,128)(2,1)}) %all-gather.22.cloned.1.call-update) | async-done | bytes 2097168 | tf_op jit(solution)/shard_map/all_gather | solution.py:315
  308.1 4.7 multiply_reduce_fusion.7
  312.8 5.9 psum.29
  318.6 6.0 multiply_reduce_fusion.8
  324.6 3.6 fusion.107
  328.3 3.3 bitcast_convert_fusion.2
  334.5 6.1 all-to-all-start.9
  347.5 58.3 %all-to-all-done.9 = bf16[8,128,1024]{2,1,0:T(8,128)(2,1)} async-done(((bf16[8,128,1024]{2,1,0:T(8,128)(2,1)}), bf16[8,128,1024]{2,1,0:T(8,128)(2,1)}, u32[]{:S(2)}, u32[]{:S(2)}) %all-to-all-start.9) | async-done | bytes 2097184 | tf_op jit(solution)/shard_map/all_to_all | solution.py:46
  405.8 4.5 all-to-all-start.1
  410.7 2.7 reduce_sum.513
  418.2 20.9 %fusion.48 = (f32[2,512,6]{1,2,0:T(8,128)}, f32[2,512,6]{1,2,0:T(8,128)}, f32[2,512,6]{1,2,0:T(8,128)}, f32[2,512,512]{2,1,0:T(8,128)}) fusion(f32[2,512,6]{1,2,0:T(8,128)S(1)} %copy-done.115, f32[2,512,512]{2,1,0:T(8,128)S(1)} %copy-done.56, f32[2,512,6]{1,2,0:T(8,128)S(1)} %copy-done.94, pred[512,512]{1,0:T(8,128)(4,1)S(1)} %copy-done.91, ...), kind=kOutput, calls=%fused_computation.68 | convolution fusion | flops 2462562304 | bytes 7725056 | tf_op jit(solution)/shard_map/transpose(jvp(stuh,suhp->sthp))/dot_general | solution.py:133
  442.2 12.6 %while.39 = (s32[]{:T(128)}, f32[2,512,2,64]{1,3,2,0:T(8,128)S(1)}, bf16[2,4096,128]{2,1,0:T(8,128)(2,1)}, s32[]{:T(128)}, bf16[2,4096,128]{1,2,0:T(8,128)(2,1)}...) while((s32[]{:T(128)}, f32[2,512,2,64]{1,3,2,0:T(8,128)S(1)}, ...), condition=%wide.region_18.19_spmd.clone, body=%wide.region_17.18_spmd.clone.sunk | while | flops 682755072 | bytes 41943416 | solution.py:398
  442.2 3.7 fusion.303
  446.2 3.9 fusion.304
  454.9 4.0 copy.279
  459.0 2.8 fusion.166
  461.8 3.3 fusion.130
  468.3 3.4 convolution_add_fusion.2
  473.9 3.6 multiply_reduce_fusion.6
  480.0 3.1 convolution_add_fusion.1
  483.1 91.3 %all-to-all-start.3 = ((bf16[2,8,512,128]{2,3,0,1:T(8,128)(2,1)}), bf16[2,8,512,128]{2,3,0,1:T(8,128)(2,1)}, u32[]{:S(2)}, u32[]{:S(2)}) async-start(bf16[2,8,512,128]{2,3,0,1:T(8,128)(2,1)} %copy.279), calls=%async_computation.3 | async-start | bytes 4194304 | tf_op jit(solution)/shard_map/all_to_all | solution.py:54
  574.6 13.8 %bitcast_add_fusion = f32[2,512,6,64]{1,3,2,0:T(8,128)S(1)} fusion(f32[2,512,6,64]{1,3,2,0:T(8,128)} %get-tuple-element.456, f32[2,512,6,64]{1,3,2,0:T(8,128)S(1)} %bitcast.414, f32[2,6,64,512]{3,2,1,0:T(8,128)S(1)} %bitcast.415, f32[2,512,6]{1,2,0:T(8,128)} %get-tuple-element.435, f32[2,512,512]{2,1,0:T(8,128)} %fusion.157, f32[2,512,6]{1,2,0:T(8,128)} %copy-done.92, ...), kind=kOutput, calls=%fused_computation.138 | convolution fusion | flops 2433220608 | bytes 8724504 | tf_op jit(solution)/shard_map/transpose(jvp(stuh,suhp->sthp))/dot_general | solution.py:133
  588.4 3.3 multiply_reduce_fusion.4
  599.9 2.8 fusion.189
  602.8 7.6 pad_add_fusion
  610.6 3.7 fusion.65
  614.3 9.2 %all-to-all-done.3 = bf16[2,8,512,128]{2,3,0,1:T(8,128)(2,1)} async-done(((bf16[2,8,512,128]{2,3,0,1:T(8,128)(2,1)}), bf16[2,8,512,128]{2,3,0,1:T(8,128)(2,1)}, u32[]{:S(2)}, u32[]{:S(2)}) %all-to-all-start.3) | async-done | bytes 2097184 | tf_op jit(solution)/shard_map/all_to_all | solution.py:54
  623.5 6.7 all-to-all-start.8
  630.3 6.5 add_convert_fusion
  644.3 3.4 pad_maximum_fusion.2
  647.7 7.9 all-to-all-done.8
  655.6 4.7 all-to-all-start.4
  664.9 32.4 %all-to-all-done.4 = bf16[2,4,128,1536]{3,2,0,1:T(8,128)(2,1)} async-done(((bf16[2,4,128,1536]{3,2,0,1:T(8,128)(2,1)}), bf16[2,4,128,1536]{3,2,0,1:T(8,128)(2,1)}, u32[]{:S(2)}, u32[]{:S(2)}) %all-to-all-start.4) | async-done | bytes 3145760 | tf_op jit(solution)/shard_map/all_to_all | solution.py:54
  697.2 2.7 convert_reduce_fusion
  704.6 3.3 fusion.101
  713.2 4.3 all-to-all-start.5
  718.2 42.0 %all-to-all-done.5 = bf16[8,128,896]{2,1,0:T(8,128)(2,1)} async-done(((bf16[8,128,896]{2,1,0:T(8,128)(2,1)}), bf16[8,128,896]{2,1,0:T(8,128)(2,1)}, u32[]{:S(2)}, u32[]{:S(2)}) %all-to-all-start.5) | async-done | bytes 1835040 | tf_op jit(solution)/shard_map/all_to_all | solution.py:46
  764.3 17.6 %all_to_all.56 = bf16[4,256,512]{2,1,0:T(8,128)(2,1)} all-to-all(bf16[4,256,512]{2,1,0:T(8,128)(2,1)S(1)} %bitcast.420), channel_id=1, replica_groups=mesh['seq'=8,'head'=4] {'head'}, dimensions={0} | all-to-all | bytes 2097152 | tf_op jit(solution)/shard_map/all_to_all | solution.py:46
  783.4 19.2 %all_to_all.57 = bf16[8,32,512]{2,1,0:T(8,128)(2,1)S(1)} all-to-all(bf16[8,32,512]{2,1,0:T(8,128)(2,1)S(1)} %bitcast.432), channel_id=1, replica_groups=mesh['seq'=8,'head'=4] {'seq'}, dimensions={0} | all-to-all | bytes 524288 | tf_op jit(solution)/shard_map/all_to_all | solution.py:46
  803.3 2.8 convert_element_type.237
  806.3 4.1 fusion.213
  811.8 35.6 %psum.31 = f32[8082]{0:T(1024)S(1)} all-reduce(f32[8082]{0:T(1024)S(1)} %concatenate.91), channel_id=1, replica_groups=mesh['seq'=8,'head'=4] {'seq'}, use_global_device_ids=true, to_apply=%region_50.51 | all-reduce | flops 8082 | bytes 64656 | tf_op jit(solution)/shard_map/psum | solution.py:465
  853.9 37.0 %psum.30 = f32[3072]{0:T(1024)S(1)} all-reduce(f32[3072]{0:T(1024)S(1)} %pad_maximum_fusion.9), channel_id=1, replica_groups=mesh['seq'=8,'head'=4] {'seq','head'}, use_global_device_ids=true, to_apply=%region_40.41 | all-reduce | flops 3072 | bytes 24576 | tf_op jit(solution)/shard_map/psum | solution.py:466
  892.1 4.1 convert_element_type.229
  898.0 3.2 fusion.214
  (546 shorter events, 155.2 us)
Async XLA Ops:
  7.2 239.7 %copy-start = (bf16[512,1024]{1,0:T(8,128)(2,1)S(1)}, bf16[512,1024]{1,0:T(8,128)(2,1)}, u32[]{:S(2)}) copy-start(bf16[512,1024]{1,0:T(8,128)(2,1)} %param.46) | copy-start | bytes 3145732
  7.2 74.5 %all-gather.36.cloned.1.call-start = ((), (), s32[]{:S(2)}) async-start(), calls=%async_computation.21 | async-start | bytes 1769472 | tf_op jit(solution)/shard_map/all_gather | solution.py:28
  11.4 91.1 %copy-start.5 = (bf16[2,512,1024]{2,1,0:T(8,128)(2,1)}, bf16[2,512,1024]{2,1,0:T(8,128)(2,1)S(1)}, u32[]{:S(2)}) copy-start(bf16[2,512,1024]{2,1,0:T(8,128)(2,1)S(1)} %multiply_convert_fusion) | copy-start | bytes 6291460
  14.9 7.3 copy-start.159
  14.9 7.3 copy-start.99
  14.9 7.3 copy-start.150
  16.0 8.8 copy-start.145
  16.0 8.8 copy-start.146
  17.3 7.6 collective-permute-start
  23.5 5.4 copy-start.86
  24.8 7.7 copy-start.82
  36.6 97.6 %all-gather.16.cloned.1.call-start = ((), (), s32[]{:S(2)}) async-start(), calls=%async_computation.11 | async-start | bytes 2359296 | tf_op jit(solution)/shard_map/all_gather | solution.py:212
  42.0 31.9 %copy-start.67 = (bf16[1024,128]{1,0:T(8,128)(2,1)S(1)}, bf16[1024,128]{1,0:T(8,128)(2,1)}, u32[]{:S(2)}) copy-start(bf16[1024,128]{1,0:T(8,128)(2,1)} %param.29) | copy-start | bytes 786436
  81.7 5.2 copy-start.84
  81.7 5.2 copy-start.90
  81.7 5.2 copy-start.93
  81.7 5.3 copy-start.114
  81.8 5.3 copy-start.157
  86.9 15.6 %copy-start.37 = (f32[2,512,6,64]{1,3,2,0:T(8,128)}, f32[2,512,6,64]{1,3,2,0:T(8,128)S(1)}, u32[]{:S(2)}) copy-start(f32[2,512,6,64]{1,3,2,0:T(8,128)S(1)} %fusion.149) | copy-start | bytes 4718596
  87.0 15.5 %copy-start.74 = (bf16[1024,384]{1,0:T(8,128)(2,1)S(1)}, bf16[1024,384]{1,0:T(8,128)(2,1)}, u32[]{:S(2)}) copy-start(bf16[1024,384]{1,0:T(8,128)(2,1)} %param.32) | copy-start | bytes 2359300
  145.2 30.4 %all-to-all-start = ((bf16[2,4,128,1024]{3,2,0,1:T(8,128)(2,1)}), bf16[2,4,128,1024]{3,2,0,1:T(8,128)(2,1)}, u32[]{:S(2)}, u32[]{:S(2)}) async-start(bf16[2,4,128,1024]{3,2,0,1:T(8,128)(2,1)} %copy.258), calls=%async_computation | async-start | bytes 4194304 | tf_op jit(solution)/shard_map/all_to_all | solution.py:54
  149.8 92.5 %all-gather.18.cloned.1.call-start = ((), (), s32[]{:S(2)}) async-start(), calls=%async_computation.12 | async-start | bytes 2621440 | tf_op jit(solution)/shard_map/all_gather | solution.py:290
  179.9 103.7 %copy-start.8 = (f32[2,128,1024]{2,1,0:T(8,128)}, f32[2,128,1024]{2,1,0:T(8,128)S(1)}, u32[]{:S(2)}) copy-start(f32[2,128,1024]{2,1,0:T(8,128)S(1)} %get-tuple-element.389) | copy-start | bytes 3145732
  181.0 64.6 %copy-start.64 = (bf16[1024,512]{1,0:T(8,128)(2,1)S(1)}, bf16[1024,512]{1,0:T(8,128)(2,1)}, u32[]{:S(2)}) copy-start(bf16[1024,512]{1,0:T(8,128)(2,1)} %param.44) | copy-start | bytes 3145732
  181.0 127.0 %all-gather.22.cloned.1.call-start = ((), (), s32[]{:S(2)}) async-start(), calls=%async_computation.14 | async-start | bytes 2621440 | tf_op jit(solution)/shard_map/all_gather | solution.py:315
  289.2 18.9 %copy-start.42 = (f32[2,512,384]{1,2,0:T(8,128)S(1)}, f32[2,512,384]{1,2,0:T(8,128)}, u32[]{:S(2)}) copy-start(f32[2,512,384]{1,2,0:T(8,128)} %get-tuple-element.391) | copy-start | bytes 4718596
  289.2 18.9 %copy-start.120 = (f32[384]{0:T(512)S(1)}, f32[384]{0:T(512)}, u32[]{:S(2)}) copy-start(f32[384]{0:T(512)} %convert_element_type.200) | copy-start | bytes 4612
  289.2 45.3 %all-to-all-start.10 = ((bf16[8,64,1024]{2,1,0:T(8,128)(2,1)}), bf16[8,64,1024]{2,1,0:T(8,128)(2,1)}, u32[]{:S(2)}, u32[]{:S(2)}) async-start(bf16[8,64,1024]{2,1,0:T(8,128)(2,1)} %bitcast.421), calls=%async_computation.10 | async-start | bytes 2097152 | tf_op jit(solution)/shard_map/all_to_all | solution.py:46
  294.8 23.8 %copy-start.122 = (f32[2,512]{1,0:T(2,128)S(1)}, f32[2,512]{1,0:T(2,128)}, u32[]{:S(2)}) copy-start(f32[2,512]{1,0:T(2,128)} %get-tuple-element.441) | copy-start | bytes 12292
  294.8 176.8 %all-gather.38.cloned.1.call-start = ((), (), s32[]{:S(2)}) async-start(), calls=%async_computation.22 | async-start | bytes 1769472 | tf_op jit(solution)/shard_map/all_gather | solution.py:28
  318.6 6.0 copy-start.85
  324.6 93.5 %copy-start.17 = (f32[2,512,384]{1,2,0:T(8,128)}, f32[2,512,384]{1,2,0:T(8,128)S(1)}, u32[]{:S(2)}) copy-start(f32[2,512,384]{1,2,0:T(8,128)S(1)} %get-tuple-element.384) | copy-start | bytes 4718596
  334.5 8.2 copy-start.153
  334.5 71.3 %all-to-all-start.9 = ((bf16[8,128,1024]{2,1,0:T(8,128)(2,1)}), bf16[8,128,1024]{2,1,0:T(8,128)(2,1)}, u32[]{:S(2)}, u32[]{:S(2)}) async-start(bf16[8,128,1024]{2,1,0:T(8,128)(2,1)} %pad_maximum_fusion.3), calls=%async_computation.9 | async-start | bytes 4194304 | tf_op jit(solution)/shard_map/all_to_all | solution.py:46
  340.5 462.7 %all-gather.34.cloned.1.call-start = ((), (), s32[]{:S(2)}) async-start(), calls=%async_computation.20 | async-start | bytes 1179648 | tf_op jit(solution)/shard_map/all_gather | solution.py:60
  405.8 77.3 %all-to-all-start.1 = ((bf16[2,4,128,1024]{3,2,0,1:T(8,128)(2,1)}), bf16[2,4,128,1024]{3,2,0,1:T(8,128)(2,1)}, u32[]{:S(2)}, u32[]{:S(2)}) async-start(bf16[2,4,128,1024]{3,2,0,1:T(8,128)(2,1)} %copy.259), calls=%async_computation.1 | async-start | bytes 4194304 | tf_op jit(solution)/shard_map/all_to_all | solution.py:54
  410.3 396.0 %all-gather.32.cloned.1.call-start = ((), (), s32[]{:S(2)}) async-start(), calls=%async_computation.19 | async-start | bytes 2359296 | tf_op jit(solution)/shard_map/all_gather | solution.py:60
  418.2 21.0 %copy-start.33 = (bf16[2,512,1024]{2,1,0:T(8,128)(2,1)S(1)}, bf16[2,512,1024]{2,1,0:T(8,128)(2,1)}, u32[]{:S(2)}) copy-start(bf16[2,512,1024]{2,1,0:T(8,128)(2,1)} %all-gather.22.cloned.1.call-done) | copy-start | bytes 6291460
  418.2 20.9 %copy-start.47 = (f32[2,512,2,64]{1,3,2,0:T(8,128)S(1)}, f32[2,512,2,64]{1,3,2,0:T(8,128)}, u32[]{:S(2)}) copy-start(f32[2,512,2,64]{1,3,2,0:T(8,128)} %copy-done.46) | copy-start | bytes 1572868
  418.2 20.9 %copy-start.63 = (bf16[128,1024]{1,0:T(8,128)(2,1)S(1)}, bf16[128,1024]{1,0:T(8,128)(2,1)}, u32[]{:S(2)}) copy-start(bf16[128,1024]{1,0:T(8,128)(2,1)} %param.31) | copy-start | bytes 786436
  468.3 5.3 copy-start.40
  477.5 5.6 copy-start.97
  483.1 91.4 %copy-start.18 = (f32[2,512,384]{1,2,0:T(8,128)S(1)}, f32[2,512,384]{1,2,0:T(8,128)}, u32[]{:S(2)}) copy-start(f32[2,512,384]{1,2,0:T(8,128)} %copy-done.17) | copy-start | bytes 4718596
  483.1 91.4 %copy-start.158 = (f32[6]{0:T(128)S(1)}, f32[6]{0:T(128)}, u32[]{:S(2)}) copy-start(f32[6]{0:T(128)} %param.40) | copy-start | bytes 76
  483.1 140.4 %all-to-all-start.3 = ((bf16[2,8,512,128]{2,3,0,1:T(8,128)(2,1)}), bf16[2,8,512,128]{2,3,0,1:T(8,128)(2,1)}, u32[]{:S(2)}, u32[]{:S(2)}) async-start(bf16[2,8,512,128]{2,3,0,1:T(8,128)(2,1)} %copy.279), calls=%async_computation.3 | async-start | bytes 4194304 | tf_op jit(solution)/shard_map/all_to_all | solution.py:54
  574.5 13.8 %copy-start.3 = (f32[2,515,640]{1,2,0:T(8,128)S(1)}, f32[2,515,640]{1,2,0:T(8,128)}, u32[]{:S(2)}) copy-start(f32[2,515,640]{1,2,0:T(8,128)} %copy-done.2) | copy-start | bytes 7910404
  574.5 13.8 %copy-start.12 = (f32[2,512,256]{1,2,0:T(8,128)S(1)}, f32[2,512,256]{1,2,0:T(8,128)}, u32[]{:S(2)}) copy-start(f32[2,512,256]{1,2,0:T(8,128)} %copy-done.10) | copy-start | bytes 3145732
  574.5 13.8 %copy-start.21 = (f32[2,512,384]{1,2,0:T(8,128)S(1)}, f32[2,512,384]{1,2,0:T(8,128)}, u32[]{:S(2)}) copy-start(f32[2,512,384]{1,2,0:T(8,128)} %copy-done.19) | copy-start | bytes 4718596
  574.5 13.8 %copy-start.31 = (f32[2,512,640]{1,2,0:T(8,128)S(1)}, f32[2,512,640]{1,2,0:T(8,128)}, u32[]{:S(2)}) copy-start(f32[2,512,640]{1,2,0:T(8,128)} %get-tuple-element.393) | copy-start | bytes 7864324
  574.5 13.8 %copy-start.59 = (f32[2,512,128]{1,2,0:T(8,128)S(1)}, f32[2,512,128]{1,2,0:T(8,128)}, u32[]{:S(2)}) copy-start(f32[2,512,128]{1,2,0:T(8,128)} %convolution_add_fusion.1) | copy-start | bytes 1572868
  597.0 13.3 %collective-permute-start.1 = (f32[2,3,640]{2,0,1:T(2,128)S(1)}, f32[2,3,640]{2,0,1:T(2,128)S(1)}, u32[]{:S(2)}, u32[]{:S(2)}) collective-permute-start(f32[2,3,640]{2,0,1:T(2,128)S(1)} %copy.273), channel_id=1, source_target_pairs={{4,0},{8,4},{12,8},{16,12},{20,16},{24,20},{28,24},{5,1},{9,5},{13... | collective-permute-start | bytes 46088 | tf_op jit(solution)/shard_map/ppermute | solution.py:23
  623.5 32.0 %all-to-all-start.8 = ((bf16[8,64,1024]{2,1,0:T(8,128)(2,1)}), bf16[8,64,1024]{2,1,0:T(8,128)(2,1)}, u32[]{:S(2)}, u32[]{:S(2)}) async-start(bf16[8,64,1024]{2,1,0:T(8,128)(2,1)} %bitcast.68), calls=%async_computation.8 | async-start | bytes 2097152 | tf_op jit(solution)/shard_map/all_to_all | solution.py:46
  630.3 6.5 slice-start
  647.7 14.9 %copy-start.58 = (bf16[1024,2,128]{2,1,0:T(2,128)(2,1)S(1)}, bf16[1024,2,128]{2,1,0:T(2,128)(2,1)}, u32[]{:S(2)}) copy-start(bf16[1024,2,128]{2,1,0:T(2,128)(2,1)} %param.30) | copy-start | bytes 1572868
  655.6 41.7 %all-to-all-start.4 = ((bf16[2,4,128,1536]{3,2,0,1:T(8,128)(2,1)}), bf16[2,4,128,1536]{3,2,0,1:T(8,128)(2,1)}, u32[]{:S(2)}, u32[]{:S(2)}) async-start(bf16[2,4,128,1536]{3,2,0,1:T(8,128)(2,1)} %pad_maximum_fusion.2), calls=%async_computation.4 | async-start | bytes 6291456 | tf_op jit(solution)/shard_map/all_to_all | solution.py:54
  660.2 190.3 %all-gather.30.cloned.1.call-start = ((), (), s32[]{:S(2)}) async-start(), calls=%async_computation.18 | async-start | bytes 1179648 | tf_op jit(solution)/shard_map/all_gather | solution.py:60
  662.4 229.7 %all-gather.24.cloned.1.call-start = ((), (), s32[]{:S(2)}) async-start(), calls=%async_computation.15 | async-start | bytes 2621440 | tf_op jit(solution)/shard_map/all_gather | solution.py:440
  662.8 37.2 %copy-start.112 = (f32[1024]{0:T(1024)S(1)}, f32[1024]{0:T(1024)}, u32[]{:S(2)}) copy-start(f32[1024]{0:T(1024)} %copy-done.111) | copy-start | bytes 12292
  664.9 35.1 %copy-start.81 = (bf16[1024,256]{1,0:T(8,128)(2,1)S(1)}, bf16[1024,256]{1,0:T(8,128)(2,1)}, u32[]{:S(2)}) copy-start(bf16[1024,256]{1,0:T(8,128)(2,1)} %param.34) | copy-start | bytes 1572868
  713.2 47.0 %all-to-all-start.5 = ((bf16[8,128,896]{2,1,0:T(8,128)(2,1)}), bf16[8,128,896]{2,1,0:T(8,128)(2,1)}, u32[]{:S(2)}, u32[]{:S(2)}) async-start(bf16[8,128,896]{2,1,0:T(8,128)(2,1)} %pad_maximum_fusion.4), calls=%async_computation.5 | async-start | bytes 3670016 | tf_op jit(solution)/shard_map/all_to_all | solution.py:46
  717.6 178.6 %all-gather.20.cloned.1.call-start = ((), (), s32[]{:S(2)}) async-start(), calls=%async_computation.13 | async-start | bytes 2621440 | tf_op jit(solution)/shard_map/all_gather | solution.py:297
  718.2 178.0 %all-gather.26.cloned.1.call-start = ((), (), s32[]{:S(2)}) async-start(), calls=%async_computation.16 | async-start | bytes 2064384 | tf_op jit(solution)/shard_map/all_gather | solution.py:60
  762.7 138.5 %all-gather.28.cloned.1.call-start = ((), (), s32[]{:S(2)}) async-start(), calls=%async_computation.17 | async-start | bytes 1081344 | tf_op jit(solution)/shard_map/all_gather | solution.py:445
  783.4 22.7 %copy-start.139 = (f32[384]{0:T(512)S(1)}, f32[384]{0:T(512)}, u32[]{:S(2)}) copy-start(f32[384]{0:T(512)} %get-tuple-element.383) | copy-start | bytes 4612
  (126 other events, 315.3 us)
Sparse Core Ops, SparseCore 0:
  36.8 44.9 all-gather.35
  84.3 49.8 all-gather.15
  181.2 61.1 all-gather.17
  285.5 22.5 all-gather.21
  328.4 73.7 all-gather.37
  404.2 38.2 all-gather.33
  444.5 48.0 all-gather.31
  663.8 39.3 all-gather.29
  705.3 21.3 all-gather.23
  728.7 22.5 all-gather.19
  762.8 47.6 all-gather.25
  814.1 52.5 all-gather.27

commit v2 on v1

--- a/solution.py
+++ b/solution.py
@@ -55,8 +55,34 @@
     return jnp.sum(landed.astype(jnp.float32), axis=1)
 
 
+def two_parts(values, rows):
+    flat = jnp.concatenate([part.reshape(-1) for part in values])
+    flat = jnp.pad(flat, (0, -flat.size % rows)).reshape(rows, -1)
+    high = lax.reduce_precision(flat, 8, 7)
+    return jnp.concatenate([high, flat - high], axis=1)
+
+
+def joined(columns, likes):
+    half = columns.shape[1] // 2
+    flat = (columns[:, :half] + columns[:, half:]).reshape(-1)
+    found, at = [], 0
+    for like in likes:
+        found.append(flat[at : at + like.size].reshape(like.shape))
+        at += like.size
+    return found
+
+
+def split_again(share, plain):
+    half = (share.shape[1] - plain) // 2
+    flat = share[:, plain : plain + half] + share[:, plain + half :]
+    high = lax.reduce_precision(flat, 8, 7)
+    return jnp.concatenate([share[:, :plain], high, flat - high], axis=1).astype(jnp.bfloat16)
+
+
 def summed_everywhere(value, axis):
-    share = summed_share(value, axis).astype(jnp.bfloat16)
+    share = lax.psum_scatter(
+        value.astype(jnp.bfloat16), axis, scatter_dimension=0, tiled=True
+    )
     return lax.all_gather(share, axis, axis=0, tiled=True).astype(jnp.float32)
 
 
@@ -223,36 +249,35 @@
             start + jnp.arange(key_block, dtype=jnp.int32),
         )
 
-    def first_pass(index, carry):
-        peak, total = carry
+    def forward_pass(index, carry):
+        peak, total, summed = carry
         keys, values, key_pos = key_piece(index)
         scores = block_scores(queries, keys, query_pos, key_pos, factor)
         new_peak = jnp.maximum(peak, jnp.max(scores, axis=-1))
-        total = total * jnp.exp(peak - new_peak) + jnp.sum(
-            jnp.exp(scores - new_peak[..., None]), axis=-1
+        kept = jnp.exp(peak - new_peak)
+        terms = jnp.exp(scores - new_peak[..., None])
+        total = total * kept + jnp.sum(terms, axis=-1)
+        summed = summed * kept[..., None] + jnp.einsum(
+            "shqk,skd->shqd",
+            terms.astype(jnp.bfloat16),
+            values,
+            preferred_element_type=jnp.float32,
         )
-        return (new_peak, total)
+        return (new_peak, total, summed)
 
     start_peak = jnp.full((sequences, heads_here, rows), MASKED, jnp.float32)
-    peak, total = lax.fori_loop(
-        0, blocks_needed, first_pass, (start_peak, jnp.zeros_like(start_peak))
-    )
-    log_total = peak + jnp.log(total)
-
-    def second_pass(index, summed):
-        keys, values, key_pos = key_piece(index)
-        scores = block_scores(queries, keys, query_pos, key_pos, factor)
-        probs = jnp.exp(scores - log_total[..., None]).astype(jnp.bfloat16)
-        return summed + jnp.einsum(
-            "shqk,skd->sqhd", probs, values, preferred_element_type=jnp.float32
-        )
-
-    attended_float = lax.fori_loop(
+    peak, total, summed = lax.fori_loop(
         0,
         blocks_needed,
-        second_pass,
-        jnp.zeros((sequences, rows, heads_here, head_dim), jnp.float32),
-    )
+        forward_pass,
+        (
+            start_peak,
+            jnp.zeros_like(start_peak),
+            jnp.zeros((sequences, heads_here, rows, head_dim), jnp.float32),
+        ),
+    )
+    log_total = peak + jnp.log(total)
+    attended_float = (summed / total[..., None]).transpose(0, 2, 1, 3)
     attended = attended_float.astype(jnp.bfloat16).reshape(sequences, rows, heads_here * head_dim)
     zgate = matmul(normalized_input, zgate_weight)
     inner = jnp.concatenate(
@@ -292,7 +317,9 @@
     up = matmul(normed_two, up_weight)
     activated = (jax.nn.silu(gate) * up).astype(jnp.bfloat16)
     feed_part = matmul(activated, down_weight)
-    feed_own = summed_rows(feed_part, "head")
+    feed_own = lax.psum_scatter(
+        feed_part.astype(jnp.bfloat16), "head", scatter_dimension=1, tiled=True
+    ).astype(jnp.float32)
     output_own = (hidden_rows + feed_own).astype(jnp.bfloat16)
     output = lax.all_gather(output_own, "head", axis=1, tiled=True)
     act_grad = matmul_back(grad_output, down_weight)
@@ -438,13 +465,6 @@
     input_norm_grad, grad_gain_one = norm_one_pull(normed_grad)
     input_rows_grad = (hidden_grad + input_norm_grad).astype(jnp.bfloat16)
     grad_input = lax.all_gather(input_rows_grad, "head", axis=1, tiled=True).astype(jnp.float32)
-    last_sums = summed_everywhere(
-        jnp.concatenate([grad_zgate, grad_inner, grad_query], axis=1), "seq"
-    )
-    shared_part = summed_share(summed_share(grad_shared, "head"), "seq").astype(jnp.bfloat16)
-    shared_sum = lax.all_gather(
-        shared_part, ("head", "seq"), axis=0, tiled=True
-    ).astype(jnp.float32)
     own_small = [
         grad_step,
         conv_grad[:, :inner_width],
@@ -455,32 +475,44 @@
     ]
     all_small = [grad_gain_one, grad_gain_two, conv_grad[:, inner_width:]]
 
-    def unpacked(flat, likes):
-        found, at = [], 0
-        for like in likes:
-            found.append(flat[at : at + like.size].reshape(like.shape))
-            at += like.size
-        return found
-
-    own_flat = lax.psum(jnp.concatenate([part.reshape(-1) for part in own_small]), "seq")
-    all_flat = lax.psum(
-        jnp.concatenate([part.reshape(-1) for part in all_small]), ("seq", "head")
-    )
-    grad_step, conv_inner_grad, grad_step_bias, grad_decay_log, grad_skip, grad_gain_ssm = unpacked(
-        own_flat, own_small
-    )
-    grad_gain_one, grad_gain_two, conv_state_grad = unpacked(all_flat, all_small)
+    plain = 2 * inner_width + grad_query.shape[1]
+    last_share = summed_share(
+        jnp.concatenate(
+            [grad_zgate, grad_inner, grad_query, two_parts(own_small, width)], axis=1
+        ),
+        "seq",
+    )
+    last_sums = lax.all_gather(
+        split_again(last_share, plain), "seq", axis=0, tiled=True
+    ).astype(jnp.float32)
+    shared_plain = grad_shared.shape[1]
+    shared_part = split_again(
+        summed_share(
+            jnp.concatenate([grad_shared, two_parts(all_small, width)], axis=1), "head"
+        ),
+        shared_plain,
+    )
+    shared_part = split_again(summed_share(shared_part, "seq"), shared_plain)
+    shared_sum = lax.all_gather(
+        shared_part, ("head", "seq"), axis=0, tiled=True
+    ).astype(jnp.float32)
+    grad_step, conv_inner_grad, grad_step_bias, grad_decay_log, grad_skip, grad_gain_ssm = joined(
+        last_sums[:, plain:], own_small
+    )
+    grad_gain_one, grad_gain_two, conv_state_grad = joined(
+        shared_sum[:, shared_plain:], all_small
+    )
     attended_width = heads_here * head_dim
     return (
         output,
         grad_input,
         grad_gain_one,
-        last_sums[:, 2 * inner_width :],
+        last_sums[:, 2 * inner_width : plain],
         shared_sum[:, :kv_width].reshape(keyvalue_matrix.shape),
         mixed_sums[:attended_width],
         last_sums[:, :inner_width],
         last_sums[:, inner_width : 2 * inner_width],
-        shared_sum[:, kv_width:],
+        shared_sum[:, kv_width:shared_plain],
         grad_step,
         conv_inner_grad,
         conv_state_grad,

time: 925 us -> 947 us (1.024)
  waiting for transfers between devices: 273 us -> 352 us
  blocking collectives: 170 us -> 99.9 us
  local copies, waits for them, and re-layouts: 66.9 us -> 81.9 us
  matrix products: 156 us -> 168 us
    psum x2 -> x0, blocking collectives: 72.5 us -> none  [the longest x1 37 us: on_device(): lax.psum(jnp.concatenate([part.reshape(-1) for part in all_small]), ('seq...]
    unnamed x12 -> x17, waiting for transfers between devices: 0.71 us -> 70.6 us
    all_to_all x4 -> x1, waiting for transfers between devices: 108 us -> 42.8 us  [summed_share(): landed = lax.all_to_all(pieces, axis, 0, 0)]
    reduce_scatter x0 -> x3, waiting for transfers between devices: none -> 36.8 us  [the longest x2 36.8 us: summed_everywhere(): lax.psum_scatter(value.astype(jnp.bfloat16), axis, scatter_dimension=0, t...]
    all_gather x1, waiting for transfers between devices: 0.01 us -> 32.9 us  [on_device(): lax.all_gather(shared_part, ('head', 'seq'), axis=0, tiled=True)]
    unnamed x328 -> x343, local copies, waits for them, and re-layouts: 18.4 us -> 35.3 us
    all_gather x1, waiting for transfers between devices: 61.3 us -> 73.6 us  [on_device(): normed_two = lax.all_gather(normed_two_rows, 'head', axis=1, tiled=True)]
    reduce_sum x6 -> x3, other arithmetic: 11.5 us -> 2.01 us  [summed_share(): return jnp.sum(landed.astype(jnp.float32), axis=0)]
  transfers between devices with their start and end apart: 22 -> 22, of which waited for: 10 -> 11; matrix products, arithmetic and copies ran while one was open for 28% -> 29% of each run, Pallas kernels for 0% -> 0%
where the time goes in v2:
time: 947 us; the launch traced here: 936 us
  waiting for transfers between devices  352 us (37%)
  matrix products  168 us (18%)
  starting transfers between devices  128 us (14%)
  blocking collectives  99.9 us (11%)
  other arithmetic  89.3 us (9%)
  local copies, waits for them, and re-layouts  81.9 us (9%)
  between operations  16.5 us (2%)
    all_to_all x3, starting transfers between devices, summed_rows(): landed = lax.all_to_all(pieces, axis, 1, 1)  106 us
    all_gather x1, waiting for transfers between devices, on_device(): normed_two = lax.all_gather(normed_two_rows, 'head', axis=1, tiled=True)  73.6 us
    unnamed x17, waiting for transfers between devices  70.6 us
    all_to_all x3, waiting for transfers between devices, summed_rows(): landed = lax.all_to_all(pieces, axis, 1, 1)  58.3 us
    dot_general x3, matrix products, intra(): jnp.einsum('stuh,suhp->sthp', mixing, channels, precision=HIGH_ACCURACY)  48.4 us
    all_to_all x1, waiting for transfers between devices, summed_share(): landed = lax.all_to_all(pieces, axis, 0, 0)  42.8 us
    all_to_all x2, blocking collectives, summed_share(): landed = lax.all_to_all(pieces, axis, 0, 0)  39.9 us
    reduce_scatter x2, waiting for transfers between devices, summed_everywhere(): lax.psum_scatter(value.astype(jnp.bfloat16), axis, scatter_dimension=0, t...  36.8 us
  transfers between devices with their start and end apart: 22, of which 11 were waited for; matrix products, arithmetic and copies ran while one was open for 29% of the time, Pallas kernels for 0%

profile of v2, /device:TPU:0, one launch (start us, length us, event | category | flops | bytes accessed | tf_op | source)
XLA Modules:
  0.0 936.2 jit_solution(12344213557424557465)
XLA Ops:
  17.6 4.9 collective-permute-start
  26.9 2.9 maximum_maximum_fusion
  29.9 3.4 fusion.65
  48.2 20.0 %all-gather = f32[16,1,6]{2,1,0:T(1,128)S(1)} all-gather(f32[2,1,6]{2,1,0:T(1,128)S(1)} %copy.485), channel_id=2, replica_groups=mesh['seq'=8,'head'=4] {'seq'}, dimensions={0}, use_global_device_ids=true | all-gather | bytes 432 | tf_op jit(solution)/shard_map/all_gather | solution.py:296
  73.5 4.4 fusion.160
  77.8 4.3 all-gather.36.cloned.1.call-done
  87.5 15.5 %fusion.76 = f32[2,512,6,64]{1,3,2,0:T(8,128)S(1)} fusion(f32[2,512,6,64]{1,3,2,0:T(8,128)S(1)} %bitcast.387, f32[2,512,6,64]{1,3,2,0:T(8,128)S(1)} %fusion.151, f32[2,512,6]{1,2,0:T(8,128)S(1)} %copy-done.120, f32[2,512,512]{2,1,0:T(8,128)S(1)} %copy-done.55, f32[2,512,6]{1,2,0:T(8,128)S(1)} %copy-done.98, pred[512,512]{1,0:T(8,128)(4,1)S(1)} %copy-done.94, ...), kind=kOutput, calls=%fused_computation.136 | convolution fusion | flops 2433220608 | bytes 7151640 | tf_op jit(solution)/shard_map/stuh,suhp->sthp/dot_general | solution.py:159
  103.0 2.9 multiply_reduce_fusion.11
  106.0 5.9 psum.14
  112.5 22.2 %all-gather.16.cloned.1.call-done = bf16[2,4096,128]{1,2,0:T(8,128)(2,1)} async-done(((bf16[2,512,128]{1,2,0:T(8,128)(2,1)}), bf16[2,4096,128]{1,2,0:T(8,128)(2,1)}) %all-gather.16.cloned.1.call-update) | async-done | bytes 2097168 | tf_op jit(solution)/shard_map/all_gather | solution.py:238
  134.8 7.7 while.28
  138.9 3.5 fusion.306
  147.4 4.6 all-to-all-start
  156.0 21.8 %all-to-all-done = bf16[2,4,128,1024]{3,2,0,1:T(8,128)(2,1)} async-done(((bf16[2,4,128,1024]{3,2,0,1:T(8,128)(2,1)}), bf16[2,4,128,1024]{3,2,0,1:T(8,128)(2,1)}, u32[]{:S(2)}, u32[]{:S(2)}) %all-to-all-start) | async-done | bytes 2097184 | tf_op jit(solution)/shard_map/all_to_all | solution.py:54
  184.3 73.6 %all-gather.18.cloned.1.call-done = bf16[2,512,1024]{2,1,0:T(8,128)(2,1)} async-done(((bf16[2,128,1024]{2,1,0:T(8,128)(2,1)}), bf16[2,512,1024]{2,1,0:T(8,128)(2,1)}) %all-gather.18.cloned.1.call-update) | async-done | bytes 2097168 | tf_op jit(solution)/shard_map/all_gather | solution.py:315
  257.9 3.0 fusion.125
  262.5 3.1 multiply_convert_fusion.1
  268.4 28.2 %all_to_all.35 = bf16[2,4,128,1024]{3,2,0,1:T(8,128)(2,1)S(1)} all-to-all(bf16[2,4,128,1024]{3,2,0,1:T(8,128)(2,1)S(1)} %copy.493), channel_id=1, replica_groups=mesh['seq'=8,'head'=4] {'head'}, dimensions={1} | all-to-all | bytes 4194304 | tf_op jit(solution)/shard_map/all_to_all | solution.py:54
  300.0 3.8 bitcast_convert_fusion
  304.1 3.4 bitcast_convert_fusion.1
  311.7 11.0 %all-gather.22.cloned.1.call-done = bf16[2,512,1024]{2,1,0:T(8,128)(2,1)} async-done(((bf16[2,128,1024]{2,1,0:T(8,128)(2,1)}), bf16[2,512,1024]{2,1,0:T(8,128)(2,1)}) %all-gather.22.cloned.1.call-update) | async-done | bytes 2097168 | tf_op jit(solution)/shard_map/all_gather | solution.py:342
  322.7 4.6 multiply_reduce_fusion.7
  327.3 5.9 psum.15
  333.2 5.9 multiply_reduce_fusion.8
  339.1 3.7 fusion.109
  348.8 3.8 convolution_convert_fusion
  352.7 36.8 %reduce-scatter.11.cloned.1.call-done = bf16[64,1024]{1,0:T(8,128)(2,1)} async-done(((bf16[512,1024]{1,0:T(8,128)(2,1)}), bf16[64,1024]{1,0:T(8,128)(2,1)}) %reduce-scatter.11.cloned.1.call-update) | async-done | bytes 131088 | tf_op jit(solution)/shard_map/reduce_scatter | solution.py:83
  391.3 69.3 %reduce-scatter.13.cloned.1.call-done = bf16[128,1024]{1,0:T(8,128)(2,1)} async-done(((bf16[1024,1024]{1,0:T(8,128)(2,1)}), bf16[128,1024]{1,0:T(8,128)(2,1)}) %reduce-scatter.13.cloned.1.call-update) | async-done | bytes 262160
  464.6 3.0 multiply_reduce_fusion.9
  467.7 20.9 %fusion.47 = (f32[2,512,6]{1,2,0:T(8,128)}, f32[2,512,6]{1,2,0:T(8,128)}, f32[2,512,6]{1,2,0:T(8,128)}, f32[2,512,512]{2,1,0:T(8,128)}) fusion(f32[2,512,6]{1,2,0:T(8,128)S(1)} %copy-done.121, f32[2,512,512]{2,1,0:T(8,128)S(1)} %copy-done.56, f32[2,512,6]{1,2,0:T(8,128)S(1)} %copy-done.99, pred[512,512]{1,0:T(8,128)(4,1)S(1)} %copy-done.95, ...), kind=kOutput, calls=%fused_computation.62 | convolution fusion | flops 2462562304 | bytes 7725056 | tf_op jit(solution)/shard_map/transpose(jvp(stuh,suhp->sthp))/dot_general | solution.py:159
  491.7 13.2 %while.29 = (s32[]{:T(128)}, f32[2,512,2,64]{1,3,2,0:T(8,128)S(1)}, bf16[2,4096,128]{2,1,0:T(8,128)(2,1)}, s32[]{:T(128)}, bf16[2,4096,128]{1,2,0:T(8,128)(2,1)}...) while((s32[]{:T(128)}, f32[2,512,2,64]{1,3,2,0:T(8,128)S(1)}, ...), condition=%wide.region_16.17_spmd.clone, body=%wide.region_15.16_spmd.clone.sunk | while | flops 682755072 | bytes 40796420 | solution.py:425
  491.7 3.7 fusion.314
  495.6 3.9 fusion.315
  505.0 3.8 fusion.169
  508.8 3.3 fusion.132
  512.2 3.9 copy.512
  516.1 96.1 %all-to-all-start.2 = ((bf16[2,8,512,128]{2,3,0,1:T(8,128)(2,1)}), bf16[2,8,512,128]{2,3,0,1:T(8,128)(2,1)}, u32[]{:S(2)}, u32[]{:S(2)}) async-start(bf16[2,8,512,128]{2,3,0,1:T(8,128)(2,1)} %copy.512), calls=%async_computation.3 | async-start | bytes 4194304 | tf_op jit(solution)/shard_map/all_to_all | solution.py:54
  612.3 4.7 convolution_add_fusion.2
  618.8 2.7 multiply_reduce_fusion.6
  623.0 11.9 %bitcast_add_fusion = f32[2,512,6,64]{1,3,2,0:T(8,128)S(1)} fusion(f32[2,512,6,64]{1,3,2,0:T(8,128)S(1)} %get-tuple-element.473, f32[2,512,6,64]{1,3,2,0:T(8,128)S(1)} %bitcast.395, f32[2,6,64,512]{3,2,1,0:T(8,128)S(1)} %bitcast.396, f32[2,512,6]{1,2,0:T(8,128)S(1)} %copy-done.122, f32[2,512,512]{2,1,0:T(8,128)S(1)} %copy-done.57, ...), kind=kOutput, calls=%fused_computation.132 | convolution fusion | flops 2433220608 | bytes 8724504 | tf_op jit(solution)/shard_map/transpose(jvp(stuh,suhp->sthp))/dot_general | solution.py:159
  637.6 3.3 multiply_reduce_fusion.4
  649.7 2.8 fusion.196
  652.5 7.6 pad_add_fusion
  660.3 2.6 fusion.64
  665.3 6.4 add_convert_fusion
  678.6 3.4 pad_maximum_fusion.2
  682.1 4.8 all-to-all-start.3
  687.8 36.0 %all-to-all-done.3 = bf16[2,4,128,1536]{3,2,0,1:T(8,128)(2,1)} async-done(((bf16[2,4,128,1536]{3,2,0,1:T(8,128)(2,1)}), bf16[2,4,128,1536]{3,2,0,1:T(8,128)(2,1)}, u32[]{:S(2)}, u32[]{:S(2)}) %all-to-all-start.3) | async-done | bytes 3145760 | tf_op jit(solution)/shard_map/all_to_all | solution.py:54
  723.8 2.6 convert_reduce_fusion
  726.5 3.4 multiply_reduce_fusion.13
  730.0 3.8 fusion.114
  733.8 3.3 bitcast_convert_fusion.6
  741.8 3.3 bitcast_convert_fusion.5
  747.6 3.1 fusion.103
  751.9 14.5 %all-to-all-start.6 = ((bf16[8,128,912]{1,2,0:T(8,128)(2,1)}), bf16[8,128,912]{1,2,0:T(8,128)(2,1)}, u32[]{:S(2)}, u32[]{:S(2)}) async-start(bf16[8,128,912]{1,2,0:T(8,128)(2,1)} %fusion.194), calls=%async_computation.7 | async-start | bytes 3735552 | tf_op jit(solution)/shard_map/all_to_all | solution.py:46
  767.1 42.8 %all-to-all-done.6 = bf16[8,128,912]{1,2,0:T(8,128)(2,1)} async-done(((bf16[8,128,912]{1,2,0:T(8,128)(2,1)}), bf16[8,128,912]{1,2,0:T(8,128)(2,1)}, u32[]{:S(2)}, u32[]{:S(2)}) %all-to-all-start.6) | async-done | bytes 1867808 | tf_op jit(solution)/shard_map/all_to_all | solution.py:46
  815.2 17.0 %all_to_all.36 = bf16[4,256,518]{1,2,0:T(8,128)(2,1)S(1)} all-to-all(bf16[4,256,518]{1,2,0:T(8,128)(2,1)S(1)} %pad_maximum_fusion.4), channel_id=1, replica_groups=mesh['seq'=8,'head'=4] {'head'}, dimensions={0} | all-to-all | bytes 2121728 | tf_op jit(solution)/shard_map/all_to_all | solution.py:46
  833.0 22.8 %all_to_all.37 = bf16[8,32,518]{2,1,0:T(8,128)(2,1)S(1)} all-to-all(bf16[8,32,518]{2,1,0:T(8,128)(2,1)S(1)} %pad_maximum_fusion.7), channel_id=1, replica_groups=mesh['seq'=8,'head'=4] {'seq'}, dimensions={0} | all-to-all | bytes 530432 | tf_op jit(solution)/shard_map/all_to_all | solution.py:46
  856.8 2.8 convert_element_type.235
  859.6 3.3 fusion.223
  862.9 2.9 copy.547
  870.8 4.1 convert_element_type.226
  880.2 3.1 copy.544
  888.5 32.9 %all-gather.26.cloned.1.call-done = bf16[1024,518]{1,0:T(8,128)(2,1)} async-done(((bf16[32,518]{1,0:T(8,128)(2,1)}), bf16[1024,518]{1,0:T(8,128)(2,1)}) %all-gather.26.cloned.1.call-update) | async-done | bytes 1060880 | tf_op jit(solution)/shard_map/all_gather | solution.py:496
  (584 shorter events, 156.3 us)
Async XLA Ops:
  7.2 255.0 %copy-start = (bf16[512,1024]{1,0:T(8,128)(2,1)S(1)}, bf16[512,1024]{1,0:T(8,128)(2,1)}, u32[]{:S(2)}) copy-start(bf16[512,1024]{1,0:T(8,128)(2,1)} %param.44) | copy-start | bytes 3145732
  7.2 75.0 %all-gather.36.cloned.1.call-start = ((), (), s32[]{:S(2)}) async-start(), calls=%async_computation.24 | async-start | bytes 1769472 | tf_op jit(solution)/shard_map/all_gather | solution.py:28
  11.3 91.7 %copy-start.6 = (bf16[2,512,1024]{2,1,0:T(8,128)(2,1)}, bf16[2,512,1024]{2,1,0:T(8,128)(2,1)S(1)}, u32[]{:S(2)}) copy-start(bf16[2,512,1024]{2,1,0:T(8,128)(2,1)S(1)} %multiply_convert_fusion) | copy-start | bytes 6291460
  15.2 7.3 copy-start.159
  15.2 7.3 copy-start.104
  15.2 7.3 copy-start.150
  16.3 9.4 %copy-start.146 = (bf16[4,384]{1,0:T(4,128)(2,1)S(1)}, bf16[4,384]{1,0:T(4,128)(2,1)}, u32[]{:S(2)}) copy-start(bf16[4,384]{1,0:T(4,128)(2,1)} %param.34) | copy-start | bytes 9220
  16.3 9.4 %copy-start.147 = (bf16[4,256]{1,0:T(4,128)(2,1)S(1)}, bf16[4,256]{1,0:T(4,128)(2,1)}, u32[]{:S(2)}) copy-start(bf16[4,256]{1,0:T(4,128)(2,1)} %param.35) | copy-start | bytes 6148
  17.6 8.2 collective-permute-start
  23.8 6.0 copy-start.91
  25.7 7.7 copy-start.86
  37.5 97.2 %all-gather.16.cloned.1.call-start = ((), (), s32[]{:S(2)}) async-start(), calls=%async_computation.11 | async-start | bytes 2359296 | tf_op jit(solution)/shard_map/all_gather | solution.py:238
  42.9 29.6 %copy-start.69 = (bf16[1024,128]{1,0:T(8,128)(2,1)S(1)}, bf16[1024,128]{1,0:T(8,128)(2,1)}, u32[]{:S(2)}) copy-start(bf16[1024,128]{1,0:T(8,128)(2,1)} %param.27) | copy-start | bytes 786436
  44.1 460.7 %copy-start.76 = (f32[512,32]{0,1:T(8,128)}, f32[512,32]{0,1:T(8,128)S(1)}, u32[]{:S(2)}) copy-start(f32[512,32]{0,1:T(8,128)S(1)} %get-tuple-element.460) | copy-start | bytes 196612
  44.1 460.7 %copy-start.78 = (f32[512,32]{0,1:T(8,128)}, f32[512,32]{0,1:T(8,128)S(1)}, u32[]{:S(2)}) copy-start(f32[512,32]{0,1:T(8,128)S(1)} %get-tuple-element.461) | copy-start | bytes 196612
  47.0 21.3 %copy-start.154 = (pred[8]{0:T(512)(128)(4,1)}, pred[8]{0:T(512)(128)(4,1)S(1)}, u32[]{:S(2)}) copy-start(pred[8]{0:T(512)(128)(4,1)S(1)} %get-tuple-element.476) | copy-start | bytes 28
  87.4 15.6 %copy-start.37 = (f32[2,512,6,64]{1,3,2,0:T(8,128)}, f32[2,512,6,64]{1,3,2,0:T(8,128)S(1)}, u32[]{:S(2)}) copy-start(f32[2,512,6,64]{1,3,2,0:T(8,128)S(1)} %fusion.151) | copy-start | bytes 4718596
  87.5 15.5 %copy-start.74 = (bf16[1024,384]{1,0:T(8,128)(2,1)S(1)}, bf16[1024,384]{1,0:T(8,128)(2,1)}, u32[]{:S(2)}) copy-start(bf16[1024,384]{1,0:T(8,128)(2,1)} %param.30) | copy-start | bytes 2359300
  112.5 30.9 %copy-start.106 = (f32[2,512]{1,0:T(2,128)}, f32[2,512]{1,0:T(2,128)S(1)}, u32[]{:S(2)}) copy-start(f32[2,512]{1,0:T(2,128)S(1)} %get-tuple-element.459) | copy-start | bytes 12292
  134.8 7.8 copy-start.63
  147.4 30.4 %all-to-all-start = ((bf16[2,4,128,1024]{3,2,0,1:T(8,128)(2,1)}), bf16[2,4,128,1024]{3,2,0,1:T(8,128)(2,1)}, u32[]{:S(2)}, u32[]{:S(2)}) async-start(bf16[2,4,128,1024]{3,2,0,1:T(8,128)(2,1)} %copy.492), calls=%async_computation | async-start | bytes 4194304 | tf_op jit(solution)/shard_map/all_to_all | solution.py:54
  152.0 105.9 %all-gather.18.cloned.1.call-start = ((), (), s32[]{:S(2)}) async-start(), calls=%async_computation.12 | async-start | bytes 2621440 | tf_op jit(solution)/shard_map/all_gather | solution.py:315
  179.9 78.0 %copy-start.65 = (bf16[1024,512]{1,0:T(8,128)(2,1)S(1)}, bf16[1024,512]{1,0:T(8,128)(2,1)}, u32[]{:S(2)}) copy-start(bf16[1024,512]{1,0:T(8,128)(2,1)} %param.42) | copy-start | bytes 3145732
  182.1 116.1 %copy-start.9 = (f32[2,128,1024]{2,1,0:T(8,128)}, f32[2,128,1024]{2,1,0:T(8,128)S(1)}, u32[]{:S(2)}) copy-start(f32[2,128,1024]{2,1,0:T(8,128)S(1)} %get-tuple-element.401) | copy-start | bytes 3145732
  184.2 138.4 %all-gather.22.cloned.1.call-start = ((), (), s32[]{:S(2)}) async-start(), calls=%async_computation.15 | async-start | bytes 2621440 | tf_op jit(solution)/shard_map/all_gather | solution.py:342
  299.9 89.5 %reduce-scatter.11.cloned.1.call-start = ((), (), s32[]{:S(2)}) async-start(), calls=%async_computation.22 | async-start | bytes 1179648 | tf_op jit(solution)/shard_map/reduce_scatter | solution.py:83
  303.9 156.7 %reduce-scatter.13.cloned.1.call-start = ((), (), s32[]{:S(2)}) async-start(), calls=%async_computation.26 | async-start | bytes 2359296
  311.6 11.1 %copy-start.42 = (f32[2,512,384]{1,2,0:T(8,128)S(1)}, f32[2,512,384]{1,2,0:T(8,128)}, u32[]{:S(2)}) copy-start(f32[2,512,384]{1,2,0:T(8,128)} %get-tuple-element.403) | copy-start | bytes 4718596
  311.6 11.1 %copy-start.107 = (f32[2,512]{1,0:T(2,128)S(1)}, f32[2,512]{1,0:T(2,128)}, u32[]{:S(2)}) copy-start(f32[2,512]{1,0:T(2,128)} %copy-done.106) | copy-start | bytes 12292
  311.6 11.1 %copy-start.128 = (f32[384]{0:T(512)S(1)}, f32[384]{0:T(512)}, u32[]{:S(2)}) copy-start(f32[384]{0:T(512)} %convert_element_type.197) | copy-start | bytes 4612
  311.6 21.5 %copy-start.129 = (f32[2,512]{1,0:T(2,128)S(1)}, f32[2,512]{1,0:T(2,128)}, u32[]{:S(2)}) copy-start(f32[2,512]{1,0:T(2,128)} %get-tuple-element.458) | copy-start | bytes 12292
  311.6 305.4 %all-gather.38.cloned.1.call-start = ((), (), s32[]{:S(2)}) async-start(), calls=%async_computation.25 | async-start | bytes 1769472 | tf_op jit(solution)/shard_map/all_gather | solution.py:28
  333.2 6.0 copy-start.89
  339.1 123.3 %copy-start.17 = (f32[2,512,384]{1,2,0:T(8,128)}, f32[2,512,384]{1,2,0:T(8,128)S(1)}, u32[]{:S(2)}) copy-start(f32[2,512,384]{1,2,0:T(8,128)S(1)} %get-tuple-element.396) | copy-start | bytes 4718596
  342.9 344.0 %reduce-scatter.9.cloned.1.call-start = ((), (), s32[]{:S(2)}) async-start(), calls=%async_computation.19 | async-start | bytes 1179648 | tf_op jit(solution)/shard_map/reduce_scatter | solution.py:83
  348.7 381.2 %reduce-scatter.7.cloned.1.call-start = ((), (), s32[]{:S(2)}) async-start(), calls=%async_computation.13 | async-start | bytes 2621440 | tf_op jit(solution)/shard_map/reduce_scatter | solution.py:320
  352.6 37.3 %copy-start.123 = (f32[8,2,6]{0,2,1:T(8,128)S(1)}, f32[8,2,6]{0,2,1:T(8,128)}, u32[]{:S(2)}) copy-start(f32[8,2,6]{0,2,1:T(8,128)} %get-tuple-element.355) | copy-start | bytes 1156
  352.6 37.4 %copy-start.153 = (pred[8]{0:T(512)(128)(4,1)S(1)}, pred[8]{0:T(512)(128)(4,1)}, u32[]{:S(2)}) copy-start(pred[8]{0:T(512)(128)(4,1)} %copy-done.152) | copy-start | bytes 28
  352.6 109.9 %copy-start.39 = (f32[2,6,64,128]{3,2,1,0:T(8,128)S(1)}, f32[2,6,64,128]{3,2,1,0:T(8,128)}, u32[]{:S(2)}) copy-start(f32[2,6,64,128]{3,2,1,0:T(8,128)} %copy-done.38) | copy-start | bytes 1179652
  352.6 109.9 %copy-start.90 = (f32[2,512,6]{1,2,0:T(8,128)S(1)}, f32[2,512,6]{1,2,0:T(8,128)}, u32[]{:S(2)}) copy-start(f32[2,512,6]{1,2,0:T(8,128)} %get-tuple-element.449) | copy-start | bytes 73732
  352.6 504.2 %all-gather.34.cloned.1.call-start = ((), (), s32[]{:S(2)}) async-start(), calls=%async_computation.23 | async-start | bytes 1179648 | tf_op jit(solution)/shard_map/all_gather | solution.py:86
  389.5 470.1 %all-gather.32.cloned.1.call-start = ((), (), s32[]{:S(2)}) async-start(), calls=%async_computation.21 | async-start | bytes 2359296 | tf_op jit(solution)/shard_map/all_gather | solution.py:86
  467.6 21.0 %copy-start.35 = (bf16[2,512,1024]{2,1,0:T(8,128)(2,1)S(1)}, bf16[2,512,1024]{2,1,0:T(8,128)(2,1)}, u32[]{:S(2)}) copy-start(bf16[2,512,1024]{2,1,0:T(8,128)(2,1)} %all-gather.22.cloned.1.call-done) | copy-start | bytes 6291460
  467.7 20.9 %copy-start.48 = (f32[2,2,512,64]{2,3,1,0:T(8,128)S(1)}, f32[2,2,512,64]{2,3,1,0:T(8,128)}, u32[]{:S(2)}) copy-start(f32[2,2,512,64]{2,3,1,0:T(8,128)} %copy-done.47) | copy-start | bytes 1572868
  467.7 20.9 %copy-start.64 = (bf16[128,1024]{1,0:T(8,128)(2,1)S(1)}, bf16[128,1024]{1,0:T(8,128)(2,1)}, u32[]{:S(2)}) copy-start(bf16[128,1024]{1,0:T(8,128)(2,1)} %param.29) | copy-start | bytes 786436
  516.1 96.1 %copy-start.54 = (f32[2,512,128]{1,2,0:T(8,128)S(1)}, f32[2,512,128]{1,2,0:T(8,128)}, u32[]{:S(2)}) copy-start(f32[2,512,128]{1,2,0:T(8,128)} %fusion.93) | copy-start | bytes 1572868
  516.1 156.2 %all-to-all-start.2 = ((bf16[2,8,512,128]{2,3,0,1:T(8,128)(2,1)}), bf16[2,8,512,128]{2,3,0,1:T(8,128)(2,1)}, u32[]{:S(2)}, u32[]{:S(2)}) async-start(bf16[2,8,512,128]{2,3,0,1:T(8,128)(2,1)} %copy.512), calls=%async_computation.3 | async-start | bytes 4194304 | tf_op jit(solution)/shard_map/all_to_all | solution.py:54
  623.0 12.0 %copy-start.36 = (f32[2,512,512]{2,1,0:T(8,128)S(1)}, f32[2,512,512]{2,1,0:T(8,128)}, u32[]{:S(2)}) copy-start(f32[2,512,512]{2,1,0:T(8,128)} %get-tuple-element.340) | copy-start | bytes 6291460
  623.0 14.5 %copy-start.13 = (f32[2,512,256]{1,2,0:T(8,128)S(1)}, f32[2,512,256]{1,2,0:T(8,128)}, u32[]{:S(2)}) copy-start(f32[2,512,256]{1,2,0:T(8,128)} %copy-done.11) | copy-start | bytes 3145732
  623.0 14.5 %copy-start.22 = (f32[2,512,384]{1,2,0:T(8,128)S(1)}, f32[2,512,384]{1,2,0:T(8,128)}, u32[]{:S(2)}) copy-start(f32[2,512,384]{1,2,0:T(8,128)} %copy-done.20) | copy-start | bytes 4718596
  623.0 14.5 %copy-start.32 = (f32[2,512,640]{1,2,0:T(8,128)S(1)}, f32[2,512,640]{1,2,0:T(8,128)}, u32[]{:S(2)}) copy-start(f32[2,512,640]{1,2,0:T(8,128)} %get-tuple-element.405) | copy-start | bytes 7864324
  623.0 14.5 %copy-start.60 = (f32[2,512,128]{1,2,0:T(8,128)S(1)}, f32[2,512,128]{1,2,0:T(8,128)}, u32[]{:S(2)}) copy-start(f32[2,512,128]{1,2,0:T(8,128)} %convolution_add_fusion.2) | copy-start | bytes 1572868
  646.3 13.8 %collective-permute-start.1 = (f32[2,3,640]{2,0,1:T(2,128)S(1)}, f32[2,3,640]{2,0,1:T(2,128)S(1)}, u32[]{:S(2)}, u32[]{:S(2)}) collective-permute-start(f32[2,3,640]{2,0,1:T(2,128)S(1)} %copy.506), channel_id=1, source_target_pairs={{4,0},{8,4},{12,8},{16,12},{20,16},{24,20},{28,24},{5,1},{9,5},{13... | collective-permute-start | bytes 46088 | tf_op jit(solution)/shard_map/ppermute | solution.py:23
  682.1 5.7 copy-start.139
  682.1 41.8 %all-to-all-start.3 = ((bf16[2,4,128,1536]{3,2,0,1:T(8,128)(2,1)}), bf16[2,4,128,1536]{3,2,0,1:T(8,128)(2,1)}, u32[]{:S(2)}, u32[]{:S(2)}) async-start(bf16[2,4,128,1536]{3,2,0,1:T(8,128)(2,1)} %pad_maximum_fusion.2), calls=%async_computation.4 | async-start | bytes 6291456 | tf_op jit(solution)/shard_map/all_to_all | solution.py:54
  686.8 180.7 %all-gather.30.cloned.1.call-start = ((), (), s32[]{:S(2)}) async-start(), calls=%async_computation.20 | async-start | bytes 1179648 | tf_op jit(solution)/shard_map/all_gather | solution.py:86
  687.4 183.3 %all-gather.20.cloned.1.call-start = ((), (), s32[]{:S(2)}) async-start(), calls=%async_computation.14 | async-start | bytes 2621440 | tf_op jit(solution)/shard_map/all_gather | solution.py:324
  687.8 38.7 %copy-start.85 = (bf16[1024,256]{1,0:T(8,128)(2,1)S(1)}, bf16[1024,256]{1,0:T(8,128)(2,1)}, u32[]{:S(2)}) copy-start(bf16[1024,256]{1,0:T(8,128)(2,1)} %param.32) | copy-start | bytes 1572868
  687.8 38.7 %copy-start.117 = (f32[1024]{0:T(1024)S(1)}, f32[1024]{0:T(1024)}, u32[]{:S(2)}) copy-start(f32[1024]{0:T(1024)} %copy-done.116) | copy-start | bytes 12292
  751.9 57.9 %all-to-all-start.6 = ((bf16[8,128,912]{1,2,0:T(8,128)(2,1)}), bf16[8,128,912]{1,2,0:T(8,128)(2,1)}, u32[]{:S(2)}, u32[]{:S(2)}) async-start(bf16[8,128,912]{1,2,0:T(8,128)(2,1)} %fusion.194), calls=%async_computation.7 | async-start | bytes 3735552 | tf_op jit(solution)/shard_map/all_to_all | solution.py:46
  766.5 46.1 %copy-start.130 = (f32[1024]{0:T(1024)S(1)}, f32[1024]{0:T(1024)}, u32[]{:S(2)}) copy-start(f32[1024]{0:T(1024)} %get-tuple-element.349) | copy-start | bytes 12292
  766.5 104.3 %all-gather.24.cloned.1.call-start = ((), (), s32[]{:S(2)}) async-start(), calls=%async_computation.16 | async-start | bytes 2621440 | tf_op jit(solution)/shard_map/all_gather | solution.py:467
  767.0 107.8 %all-gather.28.cloned.1.call-start = ((), (), s32[]{:S(2)}) async-start(), calls=%async_computation.18 | async-start | bytes 2101248 | tf_op jit(solution)/shard_map/all_gather | solution.py:485
  812.4 109.0 %all-gather.26.cloned.1.call-start = ((), (), s32[]{:S(2)}) async-start(), calls=%async_computation.17 | async-start | bytes 1351680 | tf_op jit(solution)/shard_map/all_gather | solution.py:496
  (127 other events, 347.6 us)
Sparse Core Ops, SparseCore 0:
  37.6 44.4 all-gather.35
  84.8 49.8 all-gather.15
  184.4 73.4 all-gather.17
  300.1 22.5 all-gather.21
  325.9 63.4 reduce-scatter.10
  393.8 66.7 reduce-scatter.12
  463.0 43.0 all-gather.37
  510.4 62.1 reduce-scatter.8
  575.2 30.4 reduce-scatter.6
  607.8 58.7 all-gather.33
  668.9 50.2 all-gather.31
  721.4 38.3 all-gather.29
  762.0 21.3 all-gather.19
  785.4 22.5 all-gather.23
  812.5 51.8 all-gather.27
  867.5 53.8 all-gather.25

commit v3 on v2

--- a/solution.py
+++ b/solution.py
@@ -79,10 +79,13 @@
     return jnp.concatenate([share[:, :plain], high, flat - high], axis=1).astype(jnp.bfloat16)
 
 
-def summed_everywhere(value, axis):
-    share = lax.psum_scatter(
+def early_share(value, axis):
+    return lax.psum_scatter(
         value.astype(jnp.bfloat16), axis, scatter_dimension=0, tiled=True
     )
+
+
+def gathered(share, axis):
     return lax.all_gather(share, axis, axis=0, tiled=True).astype(jnp.float32)
 
 
@@ -249,35 +252,36 @@
             start + jnp.arange(key_block, dtype=jnp.int32),
         )
 
-    def forward_pass(index, carry):
-        peak, total, summed = carry
+    def first_pass(index, carry):
+        peak, total = carry
         keys, values, key_pos = key_piece(index)
         scores = block_scores(queries, keys, query_pos, key_pos, factor)
         new_peak = jnp.maximum(peak, jnp.max(scores, axis=-1))
-        kept = jnp.exp(peak - new_peak)
-        terms = jnp.exp(scores - new_peak[..., None])
-        total = total * kept + jnp.sum(terms, axis=-1)
-        summed = summed * kept[..., None] + jnp.einsum(
-            "shqk,skd->shqd",
-            terms.astype(jnp.bfloat16),
-            values,
-            preferred_element_type=jnp.float32,
+        total = total * jnp.exp(peak - new_peak) + jnp.sum(
+            jnp.exp(scores - new_peak[..., None]), axis=-1
         )
-        return (new_peak, total, summed)
+        return (new_peak, total)
 
     start_peak = jnp.full((sequences, heads_here, rows), MASKED, jnp.float32)
-    peak, total, summed = lax.fori_loop(
+    peak, total = lax.fori_loop(
+        0, blocks_needed, first_pass, (start_peak, jnp.zeros_like(start_peak))
+    )
+    log_total = peak + jnp.log(total)
+
+    def second_pass(index, summed):
+        keys, values, key_pos = key_piece(index)
+        scores = block_scores(queries, keys, query_pos, key_pos, factor)
+        probs = jnp.exp(scores - log_total[..., None]).astype(jnp.bfloat16)
+        return summed + jnp.einsum(
+            "shqk,skd->sqhd", probs, values, preferred_element_type=jnp.float32
+        )
+
+    attended_float = lax.fori_loop(
         0,
         blocks_needed,
-        forward_pass,
-        (
-            start_peak,
-            jnp.zeros_like(start_peak),
-            jnp.zeros((sequences, heads_here, rows, head_dim), jnp.float32),
-        ),
-    )
-    log_total = peak + jnp.log(total)
-    attended_float = (summed / total[..., None]).transpose(0, 2, 1, 3)
+        second_pass,
+        jnp.zeros((sequences, rows, heads_here, head_dim), jnp.float32),
+    )
     attended = attended_float.astype(jnp.bfloat16).reshape(sequences, rows, heads_here * head_dim)
     zgate = matmul(normalized_input, zgate_weight)
     inner = jnp.concatenate(
@@ -319,9 +323,7 @@
     feed_part = matmul(activated, down_weight)
     feed_own = lax.psum_scatter(
         feed_part.astype(jnp.bfloat16), "head", scatter_dimension=1, tiled=True
-    ).astype(jnp.float32)
-    output_own = (hidden_rows + feed_own).astype(jnp.bfloat16)
-    output = lax.all_gather(output_own, "head", axis=1, tiled=True)
+    )
     act_grad = matmul_back(grad_output, down_weight)
     grad_down = weight_grad(activated, grad_output)
     gate_pull = jax.vjp(lambda gate_in, up_in: jax.nn.silu(gate_in) * up_in, gate, up)[1]
@@ -334,8 +336,8 @@
         matmul_back(gate_grad, gate_weight) + matmul_back(up_grad, up_weight), "head"
     )
     units = grad_down.shape[0]
-    down_sum = summed_everywhere(grad_down, "seq")
-    feed_sums = summed_everywhere(jnp.concatenate([grad_gate, grad_up], axis=1), "seq")
+    down_share = early_share(grad_down, "seq")
+    feed_share = early_share(jnp.concatenate([grad_gate, grad_up], axis=1), "seq")
     norm_two_pull = jax.vjp(rms_norm, hidden_rows, gain_two)[1]
     hidden_norm_grad, grad_gain_two = norm_two_pull(normed_two_grad)
     hidden_grad = own_rows(grad_output).astype(jnp.float32) + hidden_norm_grad
@@ -349,7 +351,7 @@
         .reshape(sequences, rows, heads_here, head_dim)
     )
     grad_mixer = weight_grad(ssm_normed, mixed_grad)
-    mixed_sums = summed_everywhere(jnp.concatenate([grad_output_proj, grad_mixer], axis=0), "seq")
+    mixed_share = early_share(jnp.concatenate([grad_output_proj, grad_mixer], axis=0), "seq")
     ssm_normed_grad = matmul_back(mixed_grad, mixer_weight)
     weighted = ssm_normed_grad * gain_ssm
     inner_total = lax.psum(jnp.sum(weighted * gated, axis=-1), "head")
@@ -425,6 +427,14 @@
     query_grad, keyvalue_grad_all = lax.fori_loop(
         0, blocks_needed, make_back_pass(), (query_zero, keyvalue_zero)
     )
+    down_share, feed_share, mixed_share, feed_own, unused = lax.optimization_barrier(
+        (down_share, feed_share, mixed_share, feed_own, query_grad)
+    )
+    output_own = (hidden_rows + feed_own.astype(jnp.float32)).astype(jnp.bfloat16)
+    output = lax.all_gather(output_own, "head", axis=1, tiled=True)
+    down_sum = gathered(down_share, "seq")
+    feed_sums = gathered(feed_share, "seq")
+    mixed_sums = gathered(mixed_share, "seq")
     keyvalue_grad_own = summed_rows(keyvalue_grad_all, "seq")
     key_raw_grad = rotate(keyvalue_grad_own[:, :, None, :head_dim], -positions)[:, :, 0]
     keyvalue_raw_grad = jnp.concatenate([key_raw_grad, keyvalue_grad_own[..., head_dim:]], axis=-1)

time: 947 us -> 939 us (level)
  starting transfers between devices: 128 us -> 35.3 us
  waiting for transfers between devices: 352 us -> 434 us
    all_to_all x3, starting transfers between devices: 106 us -> 12.9 us  [summed_rows(): landed = lax.all_to_all(pieces, axis, 1, 1)]
    reduce_scatter x2, waiting for transfers between devices: 36.8 us -> 94.3 us  [early_share(): lax.psum_scatter(value.astype(jnp.bfloat16), axis, scatter_dimension=0, t...]
    reduce_scatter x1, waiting for transfers between devices: 0.02 us -> 33.7 us  [on_device(): lax.psum_scatter(feed_part.astype(jnp.bfloat16), 'head', scatter_dimensio...]
    all_gather x1, waiting for transfers between devices: 73.6 us -> 56.6 us  [on_device(): normed_two = lax.all_gather(normed_two_rows, 'head', axis=1, tiled=True)]
    all_gather x2, waiting for transfers between devices: 4.35 us -> 18.1 us  [carried(): pieces = lax.all_gather(states.astype(jnp.bfloat16), axis)]
    unnamed x343 -> x296, local copies, waits for them, and re-layouts: 35.3 us -> 35.1 us
  transfers between devices with their start and end apart: 22 -> 22, of which waited for: 11 -> 13; matrix products, arithmetic and copies ran while one was open for 29% -> 29% of each run, Pallas kernels for 0% -> 0%
where the time goes in v3:
time: 939 us; the launch traced here: 929 us
  waiting for transfers between devices  434 us (46%)
  matrix products  169 us (18%)
  blocking collectives  98.5 us (10%)
  other arithmetic  88.2 us (9%)
  local copies, waits for them, and re-layouts  87.4 us (9%)
  starting transfers between devices  35.3 us (4%)
  between operations  16.2 us (2%)
    reduce_scatter x2, waiting for transfers between devices, early_share(): lax.psum_scatter(value.astype(jnp.bfloat16), axis, scatter_dimension=0, t...  94.3 us
    unnamed x17, waiting for transfers between devices  68.3 us
    all_to_all x3, waiting for transfers between devices, summed_rows(): landed = lax.all_to_all(pieces, axis, 1, 1)  57.9 us
    all_gather x1, waiting for transfers between devices, on_device(): normed_two = lax.all_gather(normed_two_rows, 'head', axis=1, tiled=True)  56.6 us
    dot_general x3, matrix products, intra(): jnp.einsum('stuh,suhp->sthp', mixing, channels, precision=HIGH_ACCURACY)  51.9 us
    all_to_all x1, waiting for transfers between devices, summed_share(): landed = lax.all_to_all(pieces, axis, 0, 0)  42.7 us
    all_to_all x2, blocking collectives, summed_share(): landed = lax.all_to_all(pieces, axis, 0, 0)  38.2 us
    unnamed x296, local copies, waits for them, and re-layouts  35.1 us
  transfers between devices with their start and end apart: 22, of which 13 were waited for; matrix products, arithmetic and copies ran while one was open for 29% of the time, Pallas kernels for 0%

profile of v3, /device:TPU:0, one launch (start us, length us, event | category | flops | bytes accessed | tf_op | source)
XLA Modules:
  0.0 929.2 jit_solution(6973546492799071220)
XLA Ops:
  17.9 4.9 collective-permute-start
  26.7 2.9 maximum_maximum_fusion
  29.6 4.2 fusion.66
  35.9 3.6 fusion.107
  51.2 20.5 %all-gather = f32[16,1,6]{2,1,0:T(1,128)S(1)} all-gather(f32[2,1,6]{2,1,0:T(1,128)S(1)} %copy.485), channel_id=2, replica_groups=mesh['seq'=8,'head'=4] {'seq'}, dimensions={0}, use_global_device_ids=true | all-gather | bytes 432 | tf_op jit(solution)/shard_map/all_gather | solution.py:300
  78.2 4.4 fusion.160
  89.6 17.3 %fusion.77 = f32[2,512,6,64]{1,3,2,0:T(8,128)S(1)} fusion(f32[2,512,6,64]{1,3,2,0:T(8,128)} %bitcast.10, f32[2,512,6,64]{1,3,2,0:T(8,128)S(1)} %fusion.152, f32[2,512,6]{1,2,0:T(8,128)S(1)} %copy-done.108, f32[2,512,512]{2,1,0:T(8,128)S(1)} %copy-done.49, f32[2,512,6]{1,2,0:T(8,128)S(1)} %copy-done.88, pred[512,512]{1,0:T(8,128)(4,1)S(1)} %copy-done.85, ...), kind=kOutput, calls=%fused_computation.142 | convolution fusion | flops 2433220608 | bytes 7151640 | tf_op jit(solution)/shard_map/stuh,suhp->sthp/dot_general | solution.py:162
  107.0 2.9 multiply_reduce_fusion.11
  109.9 5.9 psum.14
  115.9 21.0 %all-gather.16.cloned.1.call-done = bf16[2,4096,128]{1,2,0:T(8,128)(2,1)} async-done(((bf16[2,512,128]{1,2,0:T(8,128)(2,1)}), bf16[2,4096,128]{1,2,0:T(8,128)(2,1)}) %all-gather.16.cloned.1.call-update) | async-done | bytes 2097168 | tf_op jit(solution)/shard_map/all_gather | solution.py:241
  136.9 3.4 while.37
  140.4 2.9 while.38
  140.7 2.6 fusion.305
  148.3 4.6 all-to-all-start
  155.4 23.2 %all-to-all-done = bf16[2,4,128,1024]{3,2,0,1:T(8,128)(2,1)} async-done(((bf16[2,4,128,1024]{3,2,0,1:T(8,128)(2,1)}), bf16[2,4,128,1024]{3,2,0,1:T(8,128)(2,1)}, u32[]{:S(2)}, u32[]{:S(2)}) %all-to-all-start) | async-done | bytes 2097184 | tf_op jit(solution)/shard_map/all_to_all | solution.py:54
  184.1 4.5 fusion.119
  188.7 56.6 %all-gather.18.cloned.1.call-done = bf16[2,512,1024]{2,1,0:T(8,128)(2,1)} async-done(((bf16[2,128,1024]{2,1,0:T(8,128)(2,1)}), bf16[2,512,1024]{2,1,0:T(8,128)(2,1)}) %all-gather.18.cloned.1.call-update) | async-done | bytes 2097168 | tf_op jit(solution)/shard_map/all_gather | solution.py:319
  245.3 3.0 fusion.122
  248.3 3.3 fusion.69
  255.0 28.2 %all_to_all.35 = bf16[2,4,128,1024]{3,2,0,1:T(8,128)(2,1)S(1)} all-to-all(bf16[2,4,128,1024]{3,2,0,1:T(8,128)(2,1)S(1)} %copy.496), channel_id=1, replica_groups=mesh['seq'=8,'head'=4] {'head'}, dimensions={1} | all-to-all | bytes 4194304 | tf_op jit(solution)/shard_map/all_to_all | solution.py:54
  286.8 3.3 bitcast_convert_fusion.1
  298.6 3.8 convolution_convert_fusion
  302.5 7.0 all-gather.20.cloned.1.call-done
  313.9 67.5 %reduce-scatter.13.cloned.1.call-done = bf16[128,1024]{1,0:T(8,128)(2,1)} async-done(((bf16[1024,1024]{1,0:T(8,128)(2,1)}), bf16[128,1024]{1,0:T(8,128)(2,1)}) %reduce-scatter.13.cloned.1.call-update) | async-done | bytes 262160
  383.2 5.3 multiply_reduce_fusion.7
  388.5 5.6 psum.15
  394.1 5.5 multiply_reduce_fusion.8
  407.1 13.3 %while.39 = (s32[]{:T(128)}, f32[2,512,2,64]{1,3,2,0:T(8,128)S(1)}, bf16[2,4096,128]{2,1,0:T(8,128)(2,1)}, s32[]{:T(128)}, bf16[2,4096,128]{1,2,0:T(8,128)(2,1)}...) while((s32[]{:T(128)}, f32[2,512,2,64]{1,3,2,0:T(8,128)S(1)}, ...), condition=%wide.region_21.22_spmd.clone, body=%wide.region_20.21_spmd.clone.sunk | while | flops 682755072 | bytes 42893624 | solution.py:427
  407.1 3.8 fusion.313
  411.1 3.9 fusion.314
  420.4 26.8 %reduce-scatter.7.cloned.1.call-done = bf16[64,1024]{1,0:T(8,128)(2,1)} async-done(((bf16[512,1024]{1,0:T(8,128)(2,1)}), bf16[64,1024]{1,0:T(8,128)(2,1)}) %reduce-scatter.7.cloned.1.call-update) | async-done | bytes 131088 | tf_op jit(solution)/shard_map/reduce_scatter | solution.py:83
  447.2 33.7 %reduce-scatter.11.cloned.1.call-done = bf16[2,128,1024]{2,1,0:T(8,128)(2,1)} async-done(((bf16[2,512,1024]{2,1,0:T(8,128)(2,1)}), bf16[2,128,1024]{2,1,0:T(8,128)(2,1)}) %reduce-scatter.11.cloned.1.call-update) | async-done | bytes 524304 | tf_op jit(solution)/shard_map/reduce_scatter | solution.py:324
  480.9 67.5 %reduce-scatter.9.cloned.1.call-done = bf16[64,1024]{1,0:T(8,128)(2,1)} async-done(((bf16[512,1024]{1,0:T(8,128)(2,1)}), bf16[64,1024]{1,0:T(8,128)(2,1)}) %reduce-scatter.9.cloned.1.call-update) | async-done | bytes 131088 | tf_op jit(solution)/shard_map/reduce_scatter | solution.py:83
  549.6 21.5 %fusion.48 = (f32[2,512,6]{1,2,0:T(8,128)}, f32[2,512,6]{1,2,0:T(8,128)}, f32[2,512,6]{1,2,0:T(8,128)}, f32[2,512,512]{2,1,0:T(8,128)}) fusion(f32[2,512,6]{1,2,0:T(8,128)S(1)} %copy-done.108, f32[2,512,512]{2,1,0:T(8,128)} %fusion.160, f32[2,512,6]{1,2,0:T(8,128)S(1)} %copy-done.88, pred[512,512]{1,0:T(8,128)(4,1)} %iota_compare_fusion, ...), kind=kOutput, calls=%fused_computation.68 | convolution fusion | flops 2462562304 | bytes 7725056 | tf_op jit(solution)/shard_map/transpose(jvp(stuh,suhp->sthp))/dot_general | solution.py:162
  571.2 2.6 copy.515
  573.8 4.5 all-to-all-start.2
  582.6 3.1 convolution_add_fusion.2
  585.7 2.8 fusion.169
  588.4 3.3 fusion.133
  591.8 16.3 %all-gather.38.cloned.1.call-done = bf16[16,6,64,128]{3,2,1,0:T(8,128)(2,1)} async-done(((bf16[2,6,64,128]{3,2,1,0:T(8,128)(2,1)}), bf16[16,6,64,128]{3,2,1,0:T(8,128)(2,1)}) %all-gather.38.cloned.1.call-update) | async-done | bytes 1572880 | tf_op jit(solution)/shard_map/all_gather | solution.py:28
  609.9 2.7 fusion.91
  612.6 3.0 multiply_reduce_fusion.6
  618.1 13.1 %bitcast_add_fusion = f32[2,512,6,64]{1,3,2,0:T(8,128)} fusion(f32[2,512,6,64]{1,3,2,0:T(8,128)S(1)} %get-tuple-element.555, f32[2,512,6,64]{1,3,2,0:T(8,128)S(1)} %bitcast.411, f32[2,6,64,512]{3,2,1,0:T(8,128)S(1)} %bitcast.412, f32[2,512,6]{1,2,0:T(8,128)S(1)} %copy-done.109, f32[2,512,512]{2,1,0:T(8,128)S(1)} %copy-done.50, ...), kind=kOutput, calls=%fused_computation.137 | convolution fusion | flops 2433220608 | bytes 8724504 | tf_op jit(solution)/shard_map/transpose(jvp(stuh,suhp->sthp))/dot_general | solution.py:162
  631.6 5.5 multiply_reduce_fusion.4
  645.3 2.8 fusion.196
  648.1 6.8 pad_add_fusion
  655.2 2.6 fusion.65
  659.1 6.2 add_convert_fusion
  671.7 3.4 pad_maximum_fusion.2
  675.1 3.8 all-to-all-start.3
  681.1 34.7 %all-to-all-done.3 = bf16[2,4,128,1536]{3,2,0,1:T(8,128)(2,1)S(1)} async-done(((bf16[2,4,128,1536]{3,2,0,1:T(8,128)(2,1)}), bf16[2,4,128,1536]{3,2,0,1:T(8,128)(2,1)S(1)}, u32[]{:S(2)}, u32[]{:S(2)}) %all-to-all-start.3) | async-done | bytes 3145760 | tf_op jit(solution)/shard_map/all_to_all | solution.py:54
  720.7 2.7 fusion.115
  738.7 3.1 fusion.104
  743.1 14.0 %all-to-all-start.6 = ((bf16[8,128,912]{1,2,0:T(8,128)(2,1)}), bf16[8,128,912]{1,2,0:T(8,128)(2,1)}, u32[]{:S(2)}, u32[]{:S(2)}) async-start(bf16[8,128,912]{1,2,0:T(8,128)(2,1)} %fusion.194), calls=%async_computation.9 | async-start | bytes 3735552 | tf_op jit(solution)/shard_map/all_to_all | solution.py:46
  757.7 42.7 %all-to-all-done.6 = bf16[8,128,912]{1,2,0:T(8,128)(2,1)} async-done(((bf16[8,128,912]{1,2,0:T(8,128)(2,1)}), bf16[8,128,912]{1,2,0:T(8,128)(2,1)}, u32[]{:S(2)}, u32[]{:S(2)}) %all-to-all-start.6) | async-done | bytes 1867808 | tf_op jit(solution)/shard_map/all_to_all | solution.py:46
  805.9 17.0 %all_to_all.36 = bf16[4,256,518]{1,2,0:T(8,128)(2,1)S(1)} all-to-all(bf16[4,256,518]{1,2,0:T(8,128)(2,1)S(1)} %pad_maximum_fusion.4), channel_id=1, replica_groups=mesh['seq'=8,'head'=4] {'head'}, dimensions={0} | all-to-all | bytes 2121728 | tf_op jit(solution)/shard_map/all_to_all | solution.py:46
  823.7 21.2 %all_to_all.37 = bf16[8,32,518]{2,1,0:T(8,128)(2,1)S(1)} all-to-all(bf16[8,32,518]{2,1,0:T(8,128)(2,1)S(1)} %pad_maximum_fusion.7), channel_id=1, replica_groups=mesh['seq'=8,'head'=4] {'seq'}, dimensions={0} | all-to-all | bytes 530432 | tf_op jit(solution)/shard_map/all_to_all | solution.py:46
  849.2 2.8 convert_element_type.235
  852.0 3.3 fusion.223
  855.3 2.9 copy.547
  860.0 4.1 convert_element_type.227
  869.8 3.0 copy.544
  878.8 34.4 %all-gather.26.cloned.1.call-done = bf16[1024,518]{1,0:T(8,128)(2,1)} async-done(((bf16[32,518]{1,0:T(8,128)(2,1)}), bf16[1024,518]{1,0:T(8,128)(2,1)}) %all-gather.26.cloned.1.call-update) | async-done | bytes 1060880 | tf_op jit(solution)/shard_map/all_gather | solution.py:506
  919.3 3.2 copy.725
  (542 shorter events, 171.8 us)
Async XLA Ops:
  7.2 241.1 %copy-start = (bf16[1024,512]{1,0:T(8,128)(2,1)S(1)}, bf16[1024,512]{1,0:T(8,128)(2,1)}, u32[]{:S(2)}) copy-start(bf16[1024,512]{1,0:T(8,128)(2,1)} %param.44) | copy-start | bytes 3145732
  7.2 77.1 %all-gather.36.cloned.1.call-start = ((), (), s32[]{:S(2)}) async-start(), calls=%async_computation.24 | async-start | bytes 1769472 | tf_op jit(solution)/shard_map/all_gather | solution.py:28
  11.4 95.6 %copy-start.5 = (bf16[2,512,1024]{2,1,0:T(8,128)(2,1)}, bf16[2,512,1024]{2,1,0:T(8,128)(2,1)S(1)}, u32[]{:S(2)}) copy-start(bf16[2,512,1024]{2,1,0:T(8,128)(2,1)S(1)} %multiply_convert_fusion) | copy-start | bytes 6291460
  14.5 8.3 copy-start.138
  14.5 8.3 copy-start.93
  14.5 8.3 copy-start.129
  16.6 8.8 copy-start.124
  16.6 8.8 copy-start.125
  17.9 7.6 collective-permute-start
  25.4 9.8 %copy-start.75 = (f32[2,512,6]{1,2,0:T(8,128)}, f32[2,512,6]{1,2,0:T(8,128)S(1)}, u32[]{:S(2)}) copy-start(f32[2,512,6]{1,2,0:T(8,128)S(1)} %get-tuple-element.532) | copy-start | bytes 73732
  39.5 97.4 %all-gather.16.cloned.1.call-start = ((), (), s32[]{:S(2)}) async-start(), calls=%async_computation.11 | async-start | bytes 2359296 | tf_op jit(solution)/shard_map/all_gather | solution.py:241
  44.8 32.4 %copy-start.59 = (bf16[1024,128]{1,0:T(8,128)(2,1)S(1)}, bf16[1024,128]{1,0:T(8,128)(2,1)}, u32[]{:S(2)}) copy-start(bf16[1024,128]{1,0:T(8,128)(2,1)} %param.29) | copy-start | bytes 786436
  84.4 5.2 copy-start.49
  84.4 5.2 copy-start.78
  84.4 5.2 copy-start.85
  84.4 5.2 copy-start.88
  84.4 5.2 copy-start.108
  84.4 5.2 copy-start.136
  89.6 17.4 %copy-start.33 = (f32[2,512,6,64]{1,3,2,0:T(8,128)}, f32[2,512,6,64]{1,3,2,0:T(8,128)S(1)}, u32[]{:S(2)}) copy-start(f32[2,512,6,64]{1,3,2,0:T(8,128)S(1)} %fusion.152) | copy-start | bytes 4718596
  89.6 17.3 %copy-start.66 = (bf16[1024,384]{1,0:T(8,128)(2,1)S(1)}, bf16[1024,384]{1,0:T(8,128)(2,1)}, u32[]{:S(2)}) copy-start(bf16[1024,384]{1,0:T(8,128)(2,1)} %param.32) | copy-start | bytes 2359300
  148.3 30.4 %all-to-all-start = ((bf16[2,4,128,1024]{3,2,0,1:T(8,128)(2,1)}), bf16[2,4,128,1024]{3,2,0,1:T(8,128)(2,1)}, u32[]{:S(2)}, u32[]{:S(2)}) async-start(bf16[2,4,128,1024]{3,2,0,1:T(8,128)(2,1)} %copy.492), calls=%async_computation | async-start | bytes 4194304 | tf_op jit(solution)/shard_map/all_to_all | solution.py:54
  152.9 92.4 %all-gather.18.cloned.1.call-start = ((), (), s32[]{:S(2)}) async-start(), calls=%async_computation.12 | async-start | bytes 2621440 | tf_op jit(solution)/shard_map/all_gather | solution.py:319
  182.7 101.8 %copy-start.10 = (f32[2,128,1024]{2,1,0:T(8,128)}, f32[2,128,1024]{2,1,0:T(8,128)S(1)}, u32[]{:S(2)}) copy-start(f32[2,128,1024]{2,1,0:T(8,128)S(1)} %get-tuple-element.481) | copy-start | bytes 3145732
  182.7 101.8 %copy-start.110 = (f32[2,128]{1,0:T(2,128)}, f32[2,128]{1,0:T(2,128)S(1)}, u32[]{:S(2)}) copy-start(f32[2,128]{1,0:T(2,128)S(1)} %fusion.209) | copy-start | bytes 3076
  183.9 61.4 %copy-start.61 = (bf16[1024,512]{1,0:T(8,128)(2,1)S(1)}, bf16[1024,512]{1,0:T(8,128)(2,1)}, u32[]{:S(2)}) copy-start(bf16[1024,512]{1,0:T(8,128)(2,1)} %param.45) | copy-start | bytes 3145732
  183.9 125.6 %all-gather.20.cloned.1.call-start = ((), (), s32[]{:S(2)}) async-start(), calls=%async_computation.14 | async-start | bytes 2621440 | tf_op jit(solution)/shard_map/all_gather | solution.py:344
  284.5 5.6 copy-start.120
  286.7 94.6 %reduce-scatter.13.cloned.1.call-start = ((), (), s32[]{:S(2)}) async-start(), calls=%async_computation.26 | async-start | bytes 2359296
  294.2 152.9 %reduce-scatter.7.cloned.1.call-start = ((), (), s32[]{:S(2)}) async-start(), calls=%async_computation.13 | async-start | bytes 1179648 | tf_op jit(solution)/shard_map/reduce_scatter | solution.py:83
  298.3 182.6 %reduce-scatter.11.cloned.1.call-start = ((), (), s32[]{:S(2)}) async-start(), calls=%async_computation.16 | async-start | bytes 2621440 | tf_op jit(solution)/shard_map/reduce_scatter | solution.py:324
  302.4 7.0 copy-start.48
  302.4 9.2 copy-start.37
  302.5 246.0 %reduce-scatter.9.cloned.1.call-start = ((), (), s32[]{:S(2)}) async-start(), calls=%async_computation.15 | async-start | bytes 1179648 | tf_op jit(solution)/shard_map/reduce_scatter | solution.py:83
  313.8 294.3 %all-gather.38.cloned.1.call-start = ((), (), s32[]{:S(2)}) async-start(), calls=%async_computation.25 | async-start | bytes 1769472 | tf_op jit(solution)/shard_map/all_gather | solution.py:28
  383.2 10.9 %copy-start.8 = (f32[2,512,640]{1,2,0:T(8,128)S(1)}, f32[2,512,640]{1,2,0:T(8,128)}, u32[]{:S(2)}) copy-start(f32[2,512,640]{1,2,0:T(8,128)} %copy-done.7) | copy-start | bytes 7864324
  403.0 442.8 %all-gather.30.cloned.1.call-start = ((), (), s32[]{:S(2)}) async-start(), calls=%async_computation.21 | async-start | bytes 1179648 | tf_op jit(solution)/shard_map/all_gather | solution.py:89
  407.1 141.8 %copy-start.132 = (pred[8]{0:T(512)(128)(4,1)S(1)}, pred[8]{0:T(512)(128)(4,1)}, u32[]{:S(2)}) copy-start(pred[8]{0:T(512)(128)(4,1)} %copy-done.131) | copy-start | bytes 28
  548.4 300.8 %all-gather.34.cloned.1.call-start = ((), (), s32[]{:S(2)}) async-start(), calls=%async_computation.23 | async-start | bytes 1179648 | tf_op jit(solution)/shard_map/all_gather | solution.py:89
  549.6 21.5 %copy-start.32 = (bf16[2,4096,128]{2,1,0:T(8,128)(2,1)S(1)}, bf16[2,4096,128]{2,1,0:T(8,128)(2,1)}, u32[]{:S(2)}) copy-start(bf16[2,4096,128]{2,1,0:T(8,128)(2,1)} %get-tuple-element.161) | copy-start | bytes 6291460
  573.8 4.9 copy-start.79
  573.8 91.6 %all-to-all-start.2 = ((bf16[2,8,512,128]{2,3,0,1:T(8,128)(2,1)}), bf16[2,8,512,128]{2,3,0,1:T(8,128)(2,1)}, u32[]{:S(2)}, u32[]{:S(2)}) async-start(bf16[2,8,512,128]{2,3,0,1:T(8,128)(2,1)} %copy.515), calls=%async_computation.5 | async-start | bytes 4194304 | tf_op jit(solution)/shard_map/all_to_all | solution.py:54
  578.3 273.7 %all-gather.32.cloned.1.call-start = ((), (), s32[]{:S(2)}) async-start(), calls=%async_computation.22 | async-start | bytes 2359296 | tf_op jit(solution)/shard_map/all_gather | solution.py:89
  578.7 7.0 copy-start.54
  591.8 18.2 %copy-start.76 = (f32[2,512,6]{1,2,0:T(8,128)S(1)}, f32[2,512,6]{1,2,0:T(8,128)}, u32[]{:S(2)}) copy-start(f32[2,512,6]{1,2,0:T(8,128)} %copy-done.75) | copy-start | bytes 73732
  615.7 15.5 %copy-start.91 = (f32[2,512,6]{1,2,0:T(8,128)}, f32[2,512,6]{1,2,0:T(8,128)S(1)}, u32[]{:S(2)}) copy-start(f32[2,512,6]{1,2,0:T(8,128)S(1)} %get-tuple-element.554) | copy-start | bytes 73732
  618.0 13.1 %copy-start.81 = (f32[2,512,6]{1,2,0:T(8,128)S(1)}, f32[2,512,6]{1,2,0:T(8,128)}, u32[]{:S(2)}) copy-start(f32[2,512,6]{1,2,0:T(8,128)} %copy-done.80) | copy-start | bytes 73732
  618.1 13.1 %copy-start.118 = (f32[2,6]{1,0:T(2,128)S(1)}, f32[2,6]{1,0:T(2,128)}, u32[]{:S(2)}) copy-start(f32[2,6]{1,0:T(2,128)} %copy-done.117) | copy-start | bytes 148
  618.1 13.5 %copy-start.3 = (f32[2,515,640]{1,2,0:T(8,128)S(1)}, f32[2,515,640]{1,2,0:T(8,128)}, u32[]{:S(2)}) copy-start(f32[2,515,640]{1,2,0:T(8,128)} %copy-done.2) | copy-start | bytes 7910404
  631.6 5.5 copy-start.98
  631.6 5.5 copy-start.100
  631.6 5.5 copy-start.102
  631.6 5.5 copy-start.104
  641.7 13.3 %collective-permute-start.1 = (f32[2,3,640]{2,0,1:T(2,128)S(1)}, f32[2,3,640]{2,0,1:T(2,128)S(1)}, u32[]{:S(2)}, u32[]{:S(2)}) collective-permute-start(f32[2,3,640]{2,0,1:T(2,128)S(1)} %copy.509), channel_id=1, source_target_pairs={{4,0},{8,4},{12,8},{16,12},{20,16},{24,20},{28,24},{5,1},{9,5},{13... | collective-permute-start | bytes 46088 | tf_op jit(solution)/shard_map/ppermute | solution.py:23
  657.8 7.5 copy-start.38
  675.1 6.0 copy-start.119
  675.1 41.2 %copy-start.106 = (f32[1024]{0:T(1024)S(1)}, f32[1024]{0:T(1024)}, u32[]{:S(2)}) copy-start(f32[1024]{0:T(1024)} %copy-done.105) | copy-start | bytes 12292
  675.1 40.7 %all-to-all-start.3 = ((bf16[2,4,128,1536]{3,2,0,1:T(8,128)(2,1)}), bf16[2,4,128,1536]{3,2,0,1:T(8,128)(2,1)S(1)}, u32[]{:S(2)}, u32[]{:S(2)}) async-start(bf16[2,4,128,1536]{3,2,0,1:T(8,128)(2,1)} %pad_maximum_fusion.2), calls=%async_computation.6 | async-start | bytes 6291456 | tf_op jit(solution)/shard_map/all_to_all | solution.py:54
  679.0 181.0 %all-gather.24.cloned.1.call-start = ((), (), s32[]{:S(2)}) async-start(), calls=%async_computation.18 | async-start | bytes 2621440 | tf_op jit(solution)/shard_map/all_gather | solution.py:477
  728.5 5.4 copy-start.39
  743.1 57.4 %all-to-all-start.6 = ((bf16[8,128,912]{1,2,0:T(8,128)(2,1)}), bf16[8,128,912]{1,2,0:T(8,128)(2,1)}, u32[]{:S(2)}, u32[]{:S(2)}) async-start(bf16[8,128,912]{1,2,0:T(8,128)(2,1)} %fusion.194), calls=%async_computation.9 | async-start | bytes 3735552 | tf_op jit(solution)/shard_map/all_to_all | solution.py:46
  757.1 46.0 %copy-start.113 = (f32[1024]{0:T(1024)S(1)}, f32[1024]{0:T(1024)}, u32[]{:S(2)}) copy-start(f32[1024]{0:T(1024)} %get-tuple-element.419) | copy-start | bytes 12292
  757.1 106.9 %all-gather.22.cloned.1.call-start = ((), (), s32[]{:S(2)}) async-start(), calls=%async_computation.17 | async-start | bytes 2621440 | tf_op jit(solution)/shard_map/all_gather | solution.py:434
  757.7 106.4 %all-gather.28.cloned.1.call-start = ((), (), s32[]{:S(2)}) async-start(), calls=%async_computation.20 | async-start | bytes 2101248 | tf_op jit(solution)/shard_map/all_gather | solution.py:495
  803.1 110.1 %all-gather.26.cloned.1.call-start = ((), (), s32[]{:S(2)}) async-start(), calls=%async_computation.19 | async-start | bytes 1351680 | tf_op jit(solution)/shard_map/all_gather | solution.py:506
  (104 other events, 271.7 us)
Sparse Core Ops, SparseCore 0:
  39.6 44.6 all-gather.35
  87.0 49.8 all-gather.15
  184.0 61.2 all-gather.17
  286.8 22.5 all-gather.19
  313.4 67.8 reduce-scatter.12
  384.6 62.5 reduce-scatter.6
  450.4 30.4 reduce-scatter.10
  484.9 63.4 reduce-scatter.8
  550.8 57.2 all-gather.37
  610.3 51.2 all-gather.29
  664.0 39.0 all-gather.33
  705.1 49.6 all-gather.31
  757.0 20.7 all-gather.23
  779.8 22.5 all-gather.21
  805.1 50.5 all-gather.27
  859.4 53.7 all-gather.25
